TPU v7x, 256 devices: a whole 4x4x8 slice. The times are simulated.
256 devices in a mesh: row: 16 (over y, z_hi, core), col: 16 (over z_lo, x).
Axes of the slice: x: 4, y: 4, z: 8 (z_hi: 2, z_lo: 4; z = z_hi * 4 + z_lo), core: 2. Of those that a mesh axis runs over, the one named last changes fastest.
Arguments:
- object_field: float32 [2, 4096, 4096], P(None, 'row', 'col')
- probe_field: float32 [2, 128, 128], replicated, may hold values from -6 to 6
- amplitudes: float32 [2, 16, 16, 16, 128, 128], P(None, 'row', 'col'), may hold values from 0 to 2
- positions: int32 [2, 2, 16, 16, 16], P(None, None, 'row', 'col'), may hold values from 8 to 4087, as said below
- shifts: int32 [2, 2, 16, 16, 16], P(None, None, 'row', 'col'), may hold values from -8 to 8
Outputs:
- new_object: float32 [2, 4096, 4096], P(None, 'row', 'col')
- new_probe: float32 [2, 128, 128], replicated
Inputs may be any that keep to these rules, and one draw needn't show every extreme that they name: For a pattern stored at tile (r, c), positions plus shifts lie in r * 256 .. r * 256 + 255 for the first coordinate and c * 256 .. c * 256 + 255 for the second.
All inputs are finite; a program needn't handle non-finite values.
Results may differ from a plain program's by a relative error of at most 0.0003.
Values sent between devices are 32-bit elements; how exact they have to be, the bound alone decides.
A program may use at most 64 MiB of HBM per device.

v0:
```python
import functools
import math

import jax
import jax.numpy as jnp
from jax import lax
from jax.sharding import PartitionSpec as P


def padded_2(shard, sides, width):
    for axis, dim in sides:
        size, length = (lax.axis_size(axis), shard.shape[dim])
        up = [(i, (i + 1) % size) for i in range(size - 1)]
        down = [(j, i) for i, j in up]
        last = lax.slice_in_dim(shard, length - width, length, axis=dim)
        leading = lax.slice_in_dim(shard, 0, width, axis=dim)
        before = lax.ppermute(last, axis, up)
        after = lax.ppermute(leading, axis, down)
        shard = jnp.concatenate([before, shard, after], axis=dim)
    return shard


def passed_along(value, axis, steps):
    count = lax.axis_size(axis)
    leading, last = (max(0, -steps), min(count, count - steps))
    return lax.ppermute(value, axis, [(source, source + steps) for source in range(leading, last)])


def dft_tables(length):
    counter = jnp.arange(length, dtype=jnp.int32)
    product = counter[:, None] * counter[None, :] % length
    angle = product.astype(jnp.float32) * (2.0 * math.pi / length)
    factor = 1.0 / math.sqrt(length)
    return (jnp.cos(angle) * factor, jnp.sin(angle) * factor)


def left_apply(matrix, fields):
    return jnp.einsum("jk,bkl->bjl", matrix, fields, precision=lax.Precision.HIGHEST)


def right_apply(fields, matrix):
    return jnp.einsum("bjk,kl->bjl", fields, matrix, precision=lax.Precision.HIGHEST)


def transform(real_part, imag_part, cosine_table, sine_table, orient):
    half_real = left_apply(cosine_table, real_part) - orient * left_apply(sine_table, imag_part)
    half_imag = left_apply(cosine_table, imag_part) + orient * left_apply(sine_table, real_part)
    full_real = right_apply(half_real, cosine_table) - orient * right_apply(half_imag, sine_table)
    full_imag = right_apply(half_imag, cosine_table) + orient * right_apply(half_real, sine_table)
    return (full_real, full_imag)


def cut_patch(padded, row_start, col_start, width):
    first_axis = jnp.zeros((), jnp.int32)
    return lax.dynamic_slice(padded, (first_axis, row_start, col_start), (2, width, width))


def placement(starts, extent, width):
    target = jnp.arange(extent, dtype=jnp.int32)[None, :, None]
    source = jnp.arange(width, dtype=jnp.int32)[None, None, :]
    return (target == starts[:, None, None] + source).astype(jnp.float32)


def place_patches(grad_re, grad_im, rows_at, cols_at, extent_rows, extent_cols, width):
    row_place = placement(rows_at, extent_rows, width)
    col_place = placement(cols_at, extent_cols, width)
    pieces = jnp.stack([grad_re, grad_im])
    widened = jnp.einsum("cbmn,bjn->cbmj", pieces, col_place, precision=lax.Precision.HIGHEST)
    return jnp.einsum("bim,cbmj->cij", row_place, widened, precision=lax.Precision.HIGHEST)


def fetch_rim(field, half):
    return padded_2(field, (("row", 1), ("col", 2)), half)


def fold_cols(total, half, inner):
    from_right = passed_along(total[:, :, :half], "col", -1)
    from_left = passed_along(total[:, :, inner + half :], "col", 1)
    total = total.at[:, :, inner : inner + half].add(from_right)
    total = total.at[:, :, half : 2 * half].add(from_left)
    return total[:, :, half : inner + half]


def fold_rows(total, half, inner):
    from_below = passed_along(total[:, :half, :], "row", -1)
    from_above = passed_along(total[:, inner + half :, :], "row", 1)
    total = total.at[:, inner : inner + half, :].add(from_below)
    total = total.at[:, half : 2 * half, :].add(from_above)
    return total[:, half : inner + half, :]


def local(object_field, probe_field, amplitudes, positions, shifts):
    width = probe_field.shape[1]
    half = width // 2
    tile_rows = object_field.shape[1]
    tile_cols = object_field.shape[2]
    batch = amplitudes.shape[3]
    cosine_table, sine_table = dft_tables(width)
    row_anchor = lax.axis_index("row") * tile_rows
    col_anchor = lax.axis_index("col") * tile_cols
    pattern_count = batch * lax.axis_size("row") * lax.axis_size("col")
    cutter = jax.vmap(functools.partial(cut_patch, width=width), in_axes=(None, 0, 0))
    for iteration in range(amplitudes.shape[0]):
        probe_re = probe_field[0]
        probe_im = probe_field[1]
        padded = fetch_rim(object_field, half)
        rows_at = positions[0, iteration, 0, 0] + shifts[0, iteration, 0, 0] - row_anchor
        cols_at = positions[1, iteration, 0, 0] + shifts[1, iteration, 0, 0] - col_anchor
        patches = cutter(padded, rows_at, cols_at)
        obj_re = patches[:, 0]
        obj_im = patches[:, 1]
        exit_re = probe_re * obj_re - probe_im * obj_im
        exit_im = probe_re * obj_im + probe_im * obj_re
        four_re, four_im = transform(exit_re, exit_im, cosine_table, sine_table, -1.0)
        magnitude = jnp.sqrt(four_re * four_re + four_im * four_im)
        keep = 1.0 - amplitudes[iteration, 0, 0] / jnp.maximum(magnitude, 1.0)
        back_re, back_im = transform(keep * four_re, keep * four_im, cosine_table, sine_table, 1.0)
        grad_re = probe_re * back_re + probe_im * back_im
        grad_im = probe_re * back_im - probe_im * back_re
        q_real = jnp.sum(obj_re * back_re + obj_im * back_im, axis=0)
        q_imag = jnp.sum(obj_re * back_im - obj_im * back_re, axis=0)
        weight = jnp.sum(obj_re * obj_re + obj_im * obj_im, axis=0)
        terms = jnp.stack([q_real, q_imag, weight])
        grad_total = place_patches(
            grad_re, grad_im, rows_at, cols_at, padded.shape[1], padded.shape[2], width
        )
        step = 0.5 / (jnp.max(probe_re * probe_re + probe_im * probe_im) + 1e-06)
        gradient = fold_rows(fold_cols(grad_total, half, tile_cols), half, tile_rows)
        object_field = object_field - step * gradient
        summed = lax.psum(terms, ("row", "col"))
        denominator = summed[2] + 0.2 * pattern_count
        probe_field = probe_field - summed[:2] / denominator[None]
    return (object_field, probe_field)


def solution(mesh):
    in_specs = (
        P(None, "row", "col"),
        P(),
        P(None, "row", "col", None, None, None),
        P(None, None, "row", "col", None),
        P(None, None, "row", "col", None),
    )
    out_specs = (P(None, "row", "col"), P())
    return jax.shard_map(local, mesh=mesh, in_specs=in_specs, out_specs=out_specs, check_vma=False)
```

profile of v0, /device:TPU:1, one launch (start us, length us, event | category | flops | bytes accessed | tf_op | source)
XLA Modules:
  0.0 768.5 jit_solution(11827094564113023187)
XLA Ops:
  8.2 10.2 %collective-permute-start = (f32[2,64,256]{2,1,0:T(8,128)S(1)}, f32[2,64,256]{2,1,0:T(8,128)S(1)}, u32[]{:S(2)}, u32[]{:S(2)}) collective-permute-start(f32[2,64,256]{2,1,0:T(8,128)S(1)} %get-tuple-element.175), channel_id=1, source_target_pairs={{0,16},{16,32},{32,48},{48,64},{64,80},{80,96},{96,112},{112,128},... | collective-permute-start | bytes 393224 | tf_op jit(solution)/shard_map/ppermute | solution.py:17
  23.4 5.3 collective-permute-done.1
  28.9 3.1 collective-permute-start.2
  33.4 3.3 collective-permute-done.2
  36.7 3.8 collective-permute-done.3
  41.3 34.1 %while.10 = (s32[]{:T(128)}, f32[2,384,384]{2,1,0:T(8,128)S(1)}, s32[16,3]{0,1:T(4,128)S(1)}, f32[16,2,128,128]{3,2,0,1:T(8,128)S(1)}, s32[]{:T(128)}) while((s32[]{:T(128)}, f32[2,384,384]{2,1,0:T(8,128)S(1)}, s32[16,3]{0,1:T(4,128)S(1)}, f32[16,2,128,128]{3,2,0,1:T(8,128)S(1)}, s32[]{:T(128)}) %tuple.102), condition=%wide.while_cond.8, body=%wide.while_body.8.sunk | while | flops 2 | bytes 262261 | solution.py:55
  105.9 2.5 fusion.52
  108.4 2.8 fusion.5
  111.3 4.7 fusion.2
  119.6 4.0 collective-permute-start.5
  125.7 2.6 collective-permute-done.5
  132.7 236.9 %all-reduce.3.cloned.1.call-done = f32[3,128,128]{2,1,0:T(8,128)} async-done(((f32[3,128,128]{2,1,0:T(8,128)}), f32[3,128,128]{2,1,0:T(8,128)}) %all-reduce.3.cloned.1.call-update) | async-done | bytes 196624 | tf_op jit(solution)/shard_map/psum | solution.py:130
  370.7 6.0 collective-permute-start.7
  376.8 3.2 collective-permute-done.7
  380.2 8.3 %collective-permute-start.8 = (f32[2,64,256]{2,1,0:T(8,128)S(1)}, f32[2,64,256]{2,1,0:T(8,128)S(1)}, u32[]{:S(2)}, u32[]{:S(2)}) collective-permute-start(f32[2,64,256]{2,1,0:T(8,128)S(1)} %get-tuple-element.172), channel_id=1, source_target_pairs={{0,16},{16,32},{32,48},{48,64},{64,80},{80,96},{96,112},{112,128},... | collective-permute-start | bytes 393224 | tf_op jit(solution)/shard_map/ppermute | solution.py:17
  391.8 6.9 collective-permute-done.9
  398.9 2.9 collective-permute-start.10
  403.1 3.4 collective-permute-done.10
  406.4 3.8 collective-permute-done.11
  412.1 48.0 %while.11 = (s32[]{:T(128)}, f32[2,384,384]{2,1,0:T(8,128)}, s32[16,3]{0,1:T(4,128)S(1)}, f32[16,2,128,128]{3,2,0,1:T(8,128)S(1)}, s32[]{:T(128)}) while((s32[]{:T(128)}, f32[2,384,384]{2,1,0:T(8,128)}, s32[16,3]{0,1:T(4,128)S(1)}, f32[16,2,128,128]{3,2,0,1:T(8,128)S(1)}, s32[]{:T(128)}) %tuple.105), condition=%wide.while_cond.9, body=%wide.while_body.9.sunk | while | flops 2 | bytes 262261 | solution.py:55
  412.7 2.4 bitcast_dynamic-update-slice_fusion.5
  415.7 2.4 bitcast_dynamic-update-slice_fusion.5
  418.6 2.4 bitcast_dynamic-update-slice_fusion.5
  421.6 2.4 bitcast_dynamic-update-slice_fusion.5
  427.6 2.4 bitcast_dynamic-update-slice_fusion.5
  490.5 3.8 fusion.43
  495.0 4.5 fusion.10
  499.6 4.7 fusion
  505.8 4.0 collective-permute-start.13
  509.8 232.8 %all-reduce.5.cloned.1.call-done = f32[3,128,128]{2,1,0:T(8,128)} async-done(((f32[3,128,128]{2,1,0:T(8,128)}), f32[3,128,128]{2,1,0:T(8,128)}) %all-reduce.5.cloned.1.call-update) | async-done | bytes 196624 | tf_op jit(solution)/shard_map/psum | solution.py:130
  748.0 2.4 collective-permute-start.14
  751.4 7.1 collective-permute-start.15
  (201 shorter events, 165.9 us)
Async XLA Ops:
  7.2 362.4 %all-reduce.3.cloned.1.call-start = ((), (), s32[]{:S(2)}) async-start(), calls=%async_computation | async-start | bytes 393216 | tf_op jit(solution)/shard_map/psum | solution.py:130
  8.2 14.1 %collective-permute-start = (f32[2,64,256]{2,1,0:T(8,128)S(1)}, f32[2,64,256]{2,1,0:T(8,128)S(1)}, u32[]{:S(2)}, u32[]{:S(2)}) collective-permute-start(f32[2,64,256]{2,1,0:T(8,128)S(1)} %get-tuple-element.175), channel_id=1, source_target_pairs={{0,16},{16,32},{32,48},{48,64},{64,80},{80,96},{96,112},{112,128},... | collective-permute-start | bytes 393224 | tf_op jit(solution)/shard_map/ppermute | solution.py:17
  18.4 10.3 %collective-permute-start.1 = (f32[2,64,256]{2,1,0:T(8,128)S(1)}, f32[2,64,256]{2,1,0:T(8,128)S(1)}, u32[]{:S(2)}, u32[]{:S(2)}) collective-permute-start(f32[2,64,256]{2,1,0:T(8,128)S(1)} %get-tuple-element.174), channel_id=1, source_target_pairs={{16,0},{32,16},{48,32},{64,48},{80,64},{96,80},{112,96},{128,112},... | collective-permute-start | bytes 393224 | tf_op jit(solution)/shard_map/ppermute | solution.py:18
  28.9 7.8 %collective-permute-start.2 = (f32[2,384,64]{2,1,0:T(8,128)S(1)}, f32[2,384,64]{2,1,0:T(8,128)S(1)}, u32[]{:S(2)}, u32[]{:S(2)}) collective-permute-start(f32[2,384,64]{2,1,0:T(8,128)S(1)} %get-tuple-element.170), channel_id=1, source_target_pairs={{0,1},{1,2},{2,3},{3,4},{4,5},{5,6},{6,7},{7,8},{8,9},{9,10},{10,1... | collective-permute-start | bytes 589832 | tf_op jit(solution)/shard_map/ppermute | solution.py:17
  32.0 8.5 %collective-permute-start.3 = (f32[2,384,64]{2,1,0:T(8,128)S(1)}, f32[2,384,64]{2,1,0:T(8,128)S(1)}, u32[]{:S(2)}, u32[]{:S(2)}) collective-permute-start(f32[2,384,64]{2,1,0:T(8,128)S(1)} %get-tuple-element.171), channel_id=1, source_target_pairs={{1,0},{2,1},{3,2},{4,3},{5,4},{6,5},{7,6},{8,7},{9,8},{10,9},{11,1... | collective-permute-start | bytes 589832 | tf_op jit(solution)/shard_map/ppermute | solution.py:18
  87.4 2.3 copy-start.4
  111.3 6.2 copy-start.1
  116.2 8.5 %collective-permute-start.4 = (f32[2,384,64]{2,1,0:T(8,128)S(1)}, f32[2,384,64]{2,1,0:T(8,128)S(1)}, u32[]{:S(2)}, u32[]{:S(2)}) collective-permute-start(f32[2,384,64]{2,1,0:T(8,128)S(1)} %get-tuple-element.167), channel_id=1, source_target_pairs={{1,0},{2,1},{3,2},{4,3},{5,4},{6,5},{7,6},{8,7},{9,8},{10,9},{11,1... | collective-permute-start | bytes 589832 | tf_op jit(solution)/shard_map/ppermute | solution.py:26
  119.5 623.1 %all-reduce.5.cloned.1.call-start = ((), (), s32[]{:S(2)}) async-start(), calls=%async_computation.1 | async-start | bytes 393216 | tf_op jit(solution)/shard_map/psum | solution.py:130
  119.6 8.7 %collective-permute-start.5 = (f32[2,384,64]{2,1,0:T(8,128)S(1)}, f32[2,384,64]{2,1,0:T(8,128)S(1)}, u32[]{:S(2)}, u32[]{:S(2)}) collective-permute-start(f32[2,384,64]{2,1,0:T(8,128)S(1)} %get-tuple-element.166), channel_id=1, source_target_pairs={{0,1},{1,2},{2,3},{3,4},{4,5},{5,6},{6,7},{7,8},{8,9},{9,10},{10,1... | collective-permute-start | bytes 589832 | tf_op jit(solution)/shard_map/ppermute | solution.py:26
  128.4 251.6 %copy-start = (f32[2,256,256]{2,1,0:T(8,128)S(1)}, f32[2,256,256]{2,1,0:T(8,128)}, u32[]{:S(2)}) copy-start(f32[2,256,256]{2,1,0:T(8,128)} %param.21) | copy-start | bytes 1572868
  130.8 245.9 %collective-permute-start.6 = (f32[2,64,256]{2,1,0:T(8,128)S(1)}, f32[2,64,256]{2,1,0:T(8,128)S(1)}, u32[]{:S(2)}, u32[]{:S(2)}) collective-permute-start(f32[2,64,256]{2,1,0:T(8,128)S(1)} %get-tuple-element.165), channel_id=1, source_target_pairs={{16,0},{32,16},{48,32},{64,48},{80,64},{96,80},{112,96},{128,112},... | collective-permute-start | bytes 393224 | tf_op jit(solution)/shard_map/ppermute | solution.py:26
  370.4 20.0 %copy-start.2 = (f32[3,128,128]{2,1,0:T(8,128)S(1)}, f32[3,128,128]{2,1,0:T(8,128)}, u32[]{:S(2)}) copy-start(f32[3,128,128]{2,1,0:T(8,128)} %all-reduce.3.cloned.1.call-done) | copy-start | bytes 589828
  370.7 9.3 %collective-permute-start.7 = (f32[2,64,256]{2,1,0:T(8,128)S(1)}, f32[2,64,256]{2,1,0:T(8,128)S(1)}, u32[]{:S(2)}, u32[]{:S(2)}) collective-permute-start(f32[2,64,256]{2,1,0:T(8,128)S(1)} %get-tuple-element.164), channel_id=1, source_target_pairs={{0,16},{16,32},{32,48},{48,64},{64,80},{80,96},{96,112},{112,128},... | collective-permute-start | bytes 393224 | tf_op jit(solution)/shard_map/ppermute | solution.py:26
  380.2 11.6 %collective-permute-start.8 = (f32[2,64,256]{2,1,0:T(8,128)S(1)}, f32[2,64,256]{2,1,0:T(8,128)S(1)}, u32[]{:S(2)}, u32[]{:S(2)}) collective-permute-start(f32[2,64,256]{2,1,0:T(8,128)S(1)} %get-tuple-element.172), channel_id=1, source_target_pairs={{0,16},{16,32},{32,48},{48,64},{64,80},{80,96},{96,112},{112,128},... | collective-permute-start | bytes 393224 | tf_op jit(solution)/shard_map/ppermute | solution.py:17
  388.5 10.2 %collective-permute-start.9 = (f32[2,64,256]{2,1,0:T(8,128)S(1)}, f32[2,64,256]{2,1,0:T(8,128)S(1)}, u32[]{:S(2)}, u32[]{:S(2)}) collective-permute-start(f32[2,64,256]{2,1,0:T(8,128)S(1)} %get-tuple-element.173), channel_id=1, source_target_pairs={{16,0},{32,16},{48,32},{64,48},{80,64},{96,80},{112,96},{128,112},... | collective-permute-start | bytes 393224 | tf_op jit(solution)/shard_map/ppermute | solution.py:18
  398.9 7.5 collective-permute-start.10
  401.8 8.5 %collective-permute-start.11 = (f32[2,384,64]{2,1,0:T(8,128)S(1)}, f32[2,384,64]{2,1,0:T(8,128)S(1)}, u32[]{:S(2)}, u32[]{:S(2)}) collective-permute-start(f32[2,384,64]{2,1,0:T(8,128)S(1)} %get-tuple-element.169), channel_id=1, source_target_pairs={{1,0},{2,1},{3,2},{4,3},{5,4},{6,5},{7,6},{8,7},{9,8},{10,9},{11,1... | collective-permute-start | bytes 589832 | tf_op jit(solution)/shard_map/ppermute | solution.py:18
  472.1 2.2 copy-start.5
  504.5 238.9 %collective-permute-start.12 = (f32[2,384,64]{2,1,0:T(8,128)S(1)}, f32[2,384,64]{2,1,0:T(8,128)}, u32[]{:S(2)}, u32[]{:S(2)}) collective-permute-start(f32[2,384,64]{2,1,0:T(8,128)S(1)} %get-tuple-element.163), channel_id=1, source_target_pairs={{1,0},{2,1},{3,2},{4,3},{5,4},{6,5},{7,6},{8,7},{9,8},{10,9},{11,1... | collective-permute-start | bytes 589832 | tf_op jit(solution)/shard_map/ppermute | solution.py:26
  505.8 239.6 %collective-permute-start.13 = (f32[2,384,64]{2,1,0:T(8,128)S(1)}, f32[2,384,64]{2,1,0:T(8,128)S(1)}, u32[]{:S(2)}, u32[]{:S(2)}) collective-permute-start(f32[2,384,64]{2,1,0:T(8,128)S(1)} %get-tuple-element.162), channel_id=1, source_target_pairs={{0,1},{1,2},{2,3},{3,4},{4,5},{5,6},{6,7},{7,8},{8,9},{9,10},{10,1... | collective-permute-start | bytes 589832 | tf_op jit(solution)/shard_map/ppermute | solution.py:26
  743.4 7.0 copy-start.3
  748.0 10.4 %collective-permute-start.14 = (f32[2,64,256]{2,1,0:T(8,128)S(1)}, f32[2,64,256]{2,1,0:T(8,128)S(1)}, u32[]{:S(2)}, u32[]{:S(2)}) collective-permute-start(f32[2,64,256]{2,1,0:T(8,128)S(1)} %get-tuple-element.161), channel_id=1, source_target_pairs={{16,0},{32,16},{48,32},{64,48},{80,64},{96,80},{112,96},{128,112},... | collective-permute-start | bytes 393224 | tf_op jit(solution)/shard_map/ppermute | solution.py:26
  751.4 9.0 %collective-permute-start.15 = (f32[2,64,256]{2,1,0:T(8,128)S(1)}, f32[2,64,256]{2,1,0:T(8,128)S(1)}, u32[]{:S(2)}, u32[]{:S(2)}) collective-permute-start(f32[2,64,256]{2,1,0:T(8,128)S(1)} %get-tuple-element.160), channel_id=1, source_target_pairs={{0,16},{16,32},{32,48},{48,64},{64,80},{80,96},{96,112},{112,128},... | collective-permute-start | bytes 393224 | tf_op jit(solution)/shard_map/ppermute | solution.py:26
Sparse Core Ops, SparseCore 0:
  119.6 249.9 all-reduce.2
  495.2 247.3 all-reduce.4
where the time goes:
time: 784 us; the launch traced here: 769 us
  waiting for transfers between devices  505 us (64%)
  local copies, waits for them, and re-layouts  92.3 us (12%)
  matrix products  83.8 us (11%)
  starting transfers between devices  59 us (8%)
  between operations  16.6 us (2%)
  other arithmetic  10.8 us (1%)
    psum x2, waiting for transfers between devices, local(): summed = lax.psum(terms, ('row', 'col'))  470 us
    gather x96, local copies, waits for them, and re-layouts  81.1 us
    dot_general x16, matrix products, right_apply(): jnp.einsum('bjk,kl->bjl', fields, matrix, precision=lax.Precision.HIGHEST)  34.9 us
    dot_general x16, matrix products, left_apply(): jnp.einsum('jk,bkl->bjl', matrix, fields, precision=lax.Precision.HIGHEST)  32.1 us
    ppermute x8, starting transfers between devices, passed_along(): lax.ppermute(value, axis, [(source, source + steps) for source in range(l...  28 us
    ppermute x4, starting transfers between devices, padded_2(): before = lax.ppermute(last, axis, up)  24.5 us
    ppermute x4, waiting for transfers between devices, padded_2(): after = lax.ppermute(leading, axis, down)  19.9 us
  transfers between devices with their start and end apart: 18, of which 12 were waited for; matrix products, arithmetic and copies ran while one was open for 3% of the time, Pallas kernels for 0%

commit v1 on v0

v1 whole, which is shorter than its diff:
```python
import functools
import math

import jax
import jax.numpy as jnp
import ml_dtypes
import numpy as np
from jax import lax
from jax.experimental import pallas as pl
from jax.experimental.pallas import tpu as pltpu
from jax.sharding import PartitionSpec as P

MESH = pl.DeviceIdType.MESH
F32 = jnp.float32
BF16 = jnp.bfloat16

WIDTH = 128
HALF = 64
TILE = 256
PAD = TILE + 2 * HALF
BLOCKS = 4
BATCH = 16
ITERS = 2
N_ROW = 16
N_COL = 16
NX, NY, NZ = 4, 4, 8
PATTERNS = BATCH * N_ROW * N_COL
TERM_ROWS = 3 * WIDTH
CORE_ROWS = TERM_ROWS // 2
CHUNK = CORE_ROWS // NZ
CENTRE = 256
PLACED = CENTRE + WIDTH + 256


def tables():
    n = np.arange(WIDTH)
    angle = (np.outer(n, n) % WIDTH) * (2.0 * math.pi / WIDTH)
    c, s = np.cos(angle) / math.sqrt(WIDTH), np.sin(angle) / math.sqrt(WIDTH)
    parts = []
    for m in (np.block([[c, s], [-s, c]]), np.block([[c, -s], [s, c]])):
        m = m.astype(np.float32)
        high = m.astype(ml_dtypes.bfloat16)
        parts += [high, (m - high.astype(np.float32)).astype(ml_dtypes.bfloat16)]
    return np.stack(parts)


def split(x):
    high = x.astype(BF16)
    return high, (x - high.astype(F32)).astype(BF16)


def mm(a, b):
    return jnp.dot(a, b, preferred_element_type=F32)


def left_mul(high, low, x):
    xh, xl = split(x)
    return mm(high, xh) + mm(high, xl) + mm(low, xh)


def right_mul(x, high, low):
    xh, xl = split(x)
    return mm(xh, high) + mm(xl, high) + mm(xh, low)


def swap_quadrants(y):
    top = jnp.concatenate([y[:WIDTH, :WIDTH], y[WIDTH:, :WIDTH]], axis=1)
    low = jnp.concatenate([y[:WIDTH, WIDTH:], y[WIDTH:, WIDTH:]], axis=1)
    return jnp.concatenate([top, low], axis=0)


def kernel(
    obj_in, probe_in, amp_in, pos, shf, tab, new_obj, new_probe,
    obj, prb, amp, zb, grad, terms, pack, fold_row, fold_col, fold_cor,
    hpack, hbuf, core_buf, z_buf, xy_buf, total, summed,
    in_sem, halo_s, halo_r, fold_s, fold_r, core_s, core_r, z_s, z_r, xy_s, xy_r,
):
    r, c = lax.axis_index("row"), lax.axis_index("col")
    y, zh, core = r // 4, (r // 2) % 2, r % 2
    zl, x = c // 4, c % 4
    z = zh * 4 + zl
    xy = y * NX + x

    def near(dr, dc):
        return ((r + dr + N_ROW) % N_ROW, (c + dc + N_COL) % N_COL)

    def at_z(d):
        other = (z + d) % NZ
        return (y * 4 + (other // 4) * 2 + core, (other % 4) * 4 + x)

    def at_xy(d):
        other = (xy + d) % (NX * NY)
        return ((other // NX) * 4 + zh * 2 + core, zl * 4 + other % NX)

    partner = (r + 1 - 2 * core, c)
    around = [(-1, 0), (1, 0), (0, -1), (0, 1), (-1, -1), (-1, 1), (1, -1), (1, 1)]

    barrier = pltpu.get_barrier_semaphore()
    peers = [near(*d) for d in around] + [partner]
    peers += [at_z(d) for d in range(1, NZ)] + [at_xy(d) for d in range(1, NX * NY)]
    for peer in peers:
        pl.semaphore_signal(barrier, inc=1, device_id=peer, device_id_type=MESH)

    loads = [
        pltpu.make_async_copy(obj_in.at[:, :, 0:128], obj.at[:, 1, HALF:HALF + TILE], in_sem.at[0]),
        pltpu.make_async_copy(obj_in.at[:, :, 128:256], obj.at[:, 2, HALF:HALF + TILE], in_sem.at[1]),
        pltpu.make_async_copy(probe_in, prb, in_sem.at[2]),
        pltpu.make_async_copy(amp_in.at[:, 0, 0], amp, in_sem.at[3]),
    ]
    for load in loads:
        load.start()

    lane = lax.broadcasted_iota(jnp.int32, (HALF, WIDTH), 1)
    lane_full = lax.broadcasted_iota(jnp.int32, (WIDTH, WIDTH), 1)
    low_half = lane < HALF

    def remote(src, dst, ss, rs, to):
        return pltpu.make_async_remote_copy(
            src_ref=src, dst_ref=dst, send_sem=ss, recv_sem=rs, device_id=to, device_id_type=MESH
        )

    def halo_copies(h):
        src = [
            obj.at[:, 1:3, 64:128], obj.at[:, 1:3, 256:320], hpack.at[h, 0], hpack.at[h, 1],
            hpack.at[h, 0, 0:64], hpack.at[h, 1, 0:64], hpack.at[h, 0, 192:256], hpack.at[h, 1, 192:256],
        ]
        dst = [
            obj.at[:, 1:3, 320:384], obj.at[:, 1:3, 0:64], hbuf.at[h, 0, 64:320], hbuf.at[h, 1, 64:320],
            hbuf.at[h, 0, 320:384], hbuf.at[h, 1, 320:384], hbuf.at[h, 0, 0:64], hbuf.at[h, 1, 0:64],
        ]
        return [
            remote(src[i], dst[i], halo_s.at[h, i], halo_r.at[h, i], near(*around[i])) for i in range(8)
        ]

    def halo_send(h):
        copies = halo_copies(h)
        copies[0].start()
        copies[1].start()
        for t in range(4):
            rows = slice(HALF + 64 * t, HALF + 64 * t + 64)
            to = slice(64 * t, 64 * t + 64)
            hpack[h, 0, to] = jnp.where(low_half, obj[0, 1, rows], pltpu.roll(obj[1, 1, rows], 64, 1))
            hpack[h, 1, to] = jnp.where(low_half, pltpu.roll(obj[0, 2, rows], 64, 1), obj[1, 2, rows])
        for i in (4, 5, 6, 7, 2, 3):
            copies[i].start()
        return copies

    def halo_finish(h, copies):
        for copy in copies:
            copy.wait()
        for t in range(6):
            rows = slice(64 * t, 64 * t + 64)
            inside = r >= 0
            if t == 0:
                inside = r > 0
            if t == 5:
                inside = r < N_ROW - 1
            right = jnp.where(jnp.logical_and(inside, c < N_COL - 1), hbuf[h, 0, rows], 0.0)
            left = jnp.where(jnp.logical_and(inside, c > 0), hbuf[h, 1, rows], 0.0)
            obj[0, 3, rows] = right
            obj[1, 3, rows] = pltpu.roll(right, 64, 1)
            obj[0, 0, rows] = pltpu.roll(left, 64, 1)
            obj[1, 0, rows] = left

        @pl.when(r == 0)
        def _():
            obj[:, 1:3, 0:64] = jnp.zeros((2, 2, 64, WIDTH), F32)

        @pl.when(r == N_ROW - 1)
        def _():
            obj[:, 1:3, 320:384] = jnp.zeros((2, 2, 64, WIDTH), F32)

    def place_of(it, b):
        u = lax.bitwise_and(pos[0, it, 0, 0, b] + shf[0, it, 0, 0, b], TILE - 1)
        w = lax.bitwise_and(pos[1, it, 0, 0, b] + shf[1, it, 0, 0, b], TILE - 1) + HALF
        return u, lax.shift_right_arithmetic(w, 7), lax.bitwise_and(w, 127)

    def patterns(it, first, count):
        pr, pi = prb[0], prb[1]
        ah, al, bh, bl = tab[0], tab[1], tab[2], tab[3]
        patches, shifts_of, stage = [], [], []
        weight = terms[256:384]
        for p in range(count):
            fields = []
            for i in range(2):
                u, k, s = place_of(it, first + 2 * p + i)
                window = lane_full >= s
                parts = []
                for part in range(2):
                    near_block = obj[part, k, pl.ds(u, WIDTH), :]
                    next_block = obj[part, k + 1, pl.ds(u, WIDTH), :]
                    back_by = lax.bitwise_and(WIDTH - s, 127)
                    parts.append(pltpu.roll(jnp.where(window, near_block, next_block), back_by, 1))
                o_re, o_im = parts
                weight = weight + (o_re * o_re + o_im * o_im)
                patches.append((o_re, o_im))
                shifts_of.append(s)
                fields.append((pr * o_re - pi * o_im, pr * o_im + pi * o_re))
            stage.append(
                jnp.concatenate(
                    [
                        jnp.concatenate([fields[0][0], fields[1][0]], axis=1),
                        jnp.concatenate([fields[0][1], fields[1][1]], axis=1),
                    ],
                    axis=0,
                )
            )
        terms[256:384] = weight
        stage = [left_mul(ah, al, v) for v in stage]
        stage = [right_mul(swap_quadrants(v), bh, bl) for v in stage]
        kept = []
        for p, v in enumerate(stage):
            f_re, f_im = v[:, :WIDTH], v[:, WIDTH:]
            measured = amp[it, pl.ds(first + 2 * p, 2)].reshape(2 * WIDTH, WIDTH)
            keep = 1.0 - measured * lax.rsqrt(jnp.maximum(f_re * f_re + f_im * f_im, 1.0))
            kept.append(jnp.concatenate([keep * f_re, keep * f_im], axis=1))
        stage = [right_mul(v, ah, al) for v in kept]
        stage = [left_mul(bh, bl, swap_quadrants(v)) for v in stage]
        q_re, q_im = terms[0:128], terms[128:256]
        for p, v in enumerate(stage):
            for i in range(2):
                b_re = v[:WIDTH, i * WIDTH:(i + 1) * WIDTH]
                b_im = v[WIDTH:, i * WIDTH:(i + 1) * WIDTH]
                o_re, o_im = patches[2 * p + i]
                q_re = q_re + (o_re * b_re + o_im * b_im)
                q_im = q_im + (o_re * b_im - o_im * b_re)
                s = shifts_of[2 * p + i]
                b = first + 2 * p + i
                zb[b, 0, CENTRE:CENTRE + WIDTH] = pltpu.roll(pr * b_re + pi * b_im, s, 1)
                zb[b, 1, CENTRE:CENTRE + WIDTH] = pltpu.roll(pr * b_im - pi * b_re, s, 1)
        terms[0:128] = q_re
        terms[128:256] = q_im

    def gather_gradient(it, j, t):
        def add(b, acc):
            u, k, s = place_of(it, b)
            start = CENTRE - u + 64 * t
            low = jnp.where(k == j, s, WIDTH)
            high = jnp.where(k + 1 == j, s, 0)
            mine = jnp.logical_or(lane >= low, lane < high)
            return tuple(
                acc[part] + jnp.where(mine, zb[b, part, pl.ds(start, 64), :], 0.0) for part in range(2)
            )

        zero = jnp.zeros((64, WIDTH), F32)
        re, im = lax.fori_loop(0, BATCH, add, (zero, zero), unroll=4)
        if isinstance(t, int):
            rows = slice(64 * t, 64 * t + 64)
        else:
            rows = pl.ds(pl.multiple_of(64 * t, 64), 64)
        grad[0, j, rows] = re
        grad[1, j, rows] = im
        return re, im

    def fold_copies(it):
        src = [
            grad.at[:, 1:3, 0:64], grad.at[:, 1:3, 320:384], pack.at[0, 64:320], pack.at[1, 64:320],
            pack.at[0, 0:64], pack.at[1, 0:64], pack.at[0, 320:384], pack.at[1, 320:384],
        ]
        dst = [
            fold_row.at[0], fold_row.at[1], fold_col.at[0], fold_col.at[1],
            fold_cor.at[0], fold_cor.at[1], fold_cor.at[2], fold_cor.at[3],
        ]
        return [
            remote(src[i], dst[i], fold_s.at[it, i], fold_r.at[it, i], near(*around[i])) for i in range(8)
        ]

    def rim(it, t):
        re, im = gather_gradient(it, 0, t)
        rows = slice(64 * t, 64 * t + 64) if isinstance(t, int) else pl.ds(pl.multiple_of(64 * t, 64), 64)
        pack[0, rows] = jnp.where(low_half, pltpu.roll(re, 64, 1), im)
        re, im = gather_gradient(it, 3, t)
        pack[1, rows] = jnp.where(low_half, re, pltpu.roll(im, 64, 1))

    def fold_send(it):
        copies = fold_copies(it)
        for t, i in ((0, 0), (5, 1)):
            gather_gradient(it, 1, t)
            gather_gradient(it, 2, t)
            copies[i].start()
        rim(it, 0)
        copies[4].start()
        copies[5].start()
        rim(it, 5)
        copies[6].start()
        copies[7].start()

        def middle(t, carry):
            rim(it, t)
            return carry

        lax.fori_loop(1, 5, middle, 0)
        copies[2].start()
        copies[3].start()
        return copies

    def interior(it):
        def rows(t, carry):
            gather_gradient(it, 1, t)
            gather_gradient(it, 2, t)
            return carry

        lax.fori_loop(1, 5, rows, 0)

    def fold_finish(copies, step):
        for copy in copies:
            copy.wait()
        up, down, left, right = r > 0, r < N_ROW - 1, c > 0, c < N_COL - 1
        for t in range(4):
            rows = slice(HALF + 64 * t, HALF + 64 * t + 64)
            at = slice(64 * t, 64 * t + 64)
            from_left = jnp.where(left, fold_col[1, at], 0.0)
            from_right = jnp.where(right, fold_col[0, at], 0.0)
            if t == 0:
                from_left = from_left + jnp.where(jnp.logical_and(up, left), fold_cor[3], 0.0)
                from_right = from_right + jnp.where(jnp.logical_and(up, right), fold_cor[2], 0.0)
            if t == 3:
                from_left = from_left + jnp.where(jnp.logical_and(down, left), fold_cor[1], 0.0)
                from_right = from_right + jnp.where(jnp.logical_and(down, right), fold_cor[0], 0.0)
            added = [
                [jnp.where(low_half, from_left, 0.0), jnp.where(low_half, 0.0, pltpu.roll(from_right, 64, 1))],
                [jnp.where(low_half, pltpu.roll(from_left, 64, 1), 0.0), jnp.where(low_half, 0.0, from_right)],
            ]
            for part in range(2):
                for j in (1, 2):
                    g = grad[part, j, rows] + added[part][j - 1]
                    if t == 0:
                        g = g + jnp.where(up, fold_row[1, part, j - 1], 0.0)
                    if t == 3:
                        g = g + jnp.where(down, fold_row[0, part, j - 1], 0.0)
                    obj[part, j, rows] = obj[part, j, rows] - step * g

    half_at = pl.multiple_of(core * CORE_ROWS, 8)
    other_at = pl.multiple_of((1 - core) * CORE_ROWS, 8)

    def core_scatter(it):
        copy = remote(
            terms.at[pl.ds(other_at, CORE_ROWS)], core_buf.at[it], core_s.at[it, 0], core_r.at[it, 0], partner
        )
        copy.start()
        return copy

    def z_scatter(it, before):
        before.wait()
        total[it, pl.ds(half_at, CORE_ROWS)] = terms[pl.ds(half_at, CORE_ROWS)] + core_buf[it]
        copies = []
        for d in range(1, NZ):
            rows = pl.ds(pl.multiple_of(half_at + ((z + d) % NZ) * CHUNK, 8), CHUNK)
            copies.append(remote(total.at[it, rows], z_buf.at[it, d], z_s.at[it, d], z_r.at[it, d], at_z(d)))
            copies[-1].start()
        return copies

    mine_at = pl.multiple_of(half_at + z * CHUNK, 8)

    def xy_gather(it, before):
        for copy in before:
            copy.wait()
        value = total[it, pl.ds(mine_at, CHUNK)]
        for d in range(1, NZ):
            value = value + z_buf[it, d]
        xy_buf[it, xy] = value
        for d in range(1, NX * NY):
            remote(xy_buf.at[it, xy], xy_buf.at[it, xy], xy_s.at[it, d], xy_r.at[it, d], at_xy(d)).start()

    def z_gather(it):
        for d in range(1, NX * NY):
            arriving = (xy + NX * NY - d) % (NX * NY)
            remote(xy_buf.at[it, xy], xy_buf.at[it, arriving], xy_s.at[it, d], xy_r.at[it, d], at_xy(d)).wait()
        value = xy_buf[it, 0]
        for d in range(1, NX * NY):
            value = value + xy_buf[it, d]
        summed[it, pl.ds(mine_at, CHUNK)] = value
        rows = summed.at[it, pl.ds(mine_at, CHUNK)]
        for d in range(1, NZ):
            remote(rows, rows, z_s.at[it, NZ + d], z_r.at[it, NZ + d], at_z(d)).start()

    def core_gather(it):
        rows = summed.at[it, pl.ds(mine_at, CHUNK)]
        for d in range(1, NZ):
            arriving = pl.multiple_of(half_at + ((z + NZ - d) % NZ) * CHUNK, 8)
            remote(
                rows, summed.at[it, pl.ds(arriving, CHUNK)], z_s.at[it, NZ + d], z_r.at[it, NZ + d], at_z(d)
            ).wait()
        half = summed.at[it, pl.ds(half_at, CORE_ROWS)]
        remote(half, half, core_s.at[it, 1], core_r.at[it, 1], partner).start()

    def new_probe_from(it):
        half = summed.at[it, pl.ds(half_at, CORE_ROWS)]
        other = summed.at[it, pl.ds(other_at, CORE_ROWS)]
        remote(half, other, core_s.at[it, 1], core_r.at[it, 1], partner).wait()
        under = summed[it, 256:384] + 0.2 * PATTERNS
        prb[0] = prb[0] - summed[it, 0:128] / under
        prb[1] = prb[1] - summed[it, 128:256] / under

    loads[0].wait()
    loads[1].wait()
    pl.semaphore_wait(barrier, len(peers))
    copies = halo_send(0)

    def clear(b, carry):
        for part in range(2):
            zb[b, part, 0:CENTRE] = jnp.zeros((CENTRE, WIDTH), F32)
            zb[b, part, CENTRE + WIDTH:] = jnp.zeros((PLACED - CENTRE - WIDTH, WIDTH), F32)
        return carry

    lax.fori_loop(0, BATCH, clear, 0)
    loads[2].wait()
    loads[3].wait()
    halo_finish(0, copies)

    for it in range(ITERS):
        terms[...] = jnp.zeros((TERM_ROWS, WIDTH), F32)

        def some(g, carry):
            patterns(it, g * 4, 2)
            return carry

        lax.fori_loop(0, BATCH // 4, some, 0)
        power = prb[0] * prb[0] + prb[1] * prb[1]
        step = 0.5 / (jnp.max(power) + 1e-6)
        summing = core_scatter(it)
        copies = fold_send(it)
        summing = z_scatter(it, summing)
        interior(it)
        xy_gather(it, summing)
        fold_finish(copies, step)
        if it + 1 < ITERS:
            copies = halo_send(it + 1)
        else:
            for j in range(2):
                new_obj[:, :, j * 128:(j + 1) * 128] = obj[:, 1 + j, HALF:HALF + TILE]
        z_gather(it)
        core_gather(it)
        new_probe_from(it)
        if it + 1 < ITERS:
            halo_finish(it + 1, copies)
    new_probe[...] = prb[...]


def local(object_field, probe_field, amplitudes, positions, shifts):
    vmem = pl.BlockSpec(memory_space=pltpu.VMEM)
    smem = pl.BlockSpec(memory_space=pltpu.SMEM)
    hbm = pl.BlockSpec(memory_space=pl.ANY)
    dma = pltpu.SemaphoreType.DMA
    scratch = [
        pltpu.VMEM((2, BLOCKS, PAD, WIDTH), F32),
        pltpu.VMEM((2, WIDTH, WIDTH), F32),
        pltpu.VMEM((ITERS, BATCH, WIDTH, WIDTH), F32),
        pltpu.VMEM((BATCH, 2, PLACED, WIDTH), F32),
        pltpu.VMEM((2, BLOCKS, PAD, WIDTH), F32),
        pltpu.VMEM((TERM_ROWS, WIDTH), F32),
        pltpu.VMEM((2, PAD, WIDTH), F32),
        pltpu.VMEM((2, 2, 2, HALF, WIDTH), F32),
        pltpu.VMEM((2, TILE, WIDTH), F32),
        pltpu.VMEM((4, HALF, WIDTH), F32),
        pltpu.VMEM((ITERS, 2, TILE, WIDTH), F32),
        pltpu.VMEM((ITERS, 2, PAD, WIDTH), F32),
        pltpu.VMEM((ITERS, CORE_ROWS, WIDTH), F32),
        pltpu.VMEM((ITERS, NZ, CHUNK, WIDTH), F32),
        pltpu.VMEM((ITERS, NX * NY, CHUNK, WIDTH), F32),
        pltpu.VMEM((ITERS, TERM_ROWS, WIDTH), F32),
        pltpu.VMEM((ITERS, TERM_ROWS, WIDTH), F32),
        dma((4,)),
        dma((ITERS, 8)), dma((ITERS, 8)),
        dma((ITERS, 8)), dma((ITERS, 8)),
        dma((ITERS, 2)), dma((ITERS, 2)),
        dma((ITERS, 2 * NZ)), dma((ITERS, 2 * NZ)),
        dma((ITERS, NX * NY)), dma((ITERS, NX * NY)),
    ]
    return pl.pallas_call(
        kernel,
        out_shape=(
            jax.ShapeDtypeStruct((2, TILE, TILE), F32),
            jax.ShapeDtypeStruct((2, WIDTH, WIDTH), F32),
        ),
        in_specs=[hbm, hbm, hbm, smem, smem, vmem],
        out_specs=(vmem, vmem),
        scratch_shapes=scratch,
        compiler_params=pltpu.CompilerParams(
            collective_id=0, has_side_effects=True, vmem_limit_bytes=48 * 1024 * 1024
        ),
    )(object_field, probe_field, amplitudes, positions, shifts, jnp.asarray(tables()))


def solution(mesh):
    in_specs = (
        P(None, "row", "col"),
        P(),
        P(None, "row", "col", None, None, None),
        P(None, None, "row", "col", None),
        P(None, None, "row", "col", None),
    )
    out_specs = (P(None, "row", "col"), P())
    return jax.shard_map(local, mesh=mesh, in_specs=in_specs, out_specs=out_specs, check_vma=False)
```

time: 784 us -> 119 us (0.15); the launches traced: 769 us -> 118 us
  waiting for transfers between devices: 505 us -> 0 us
  Pallas kernels: 0 us -> 110 us
  local copies, waits for them, and re-layouts: 92.3 us -> 7.38 us
  matrix products: 83.8 us -> 0 us
  starting transfers between devices: 59 us -> 0 us
  between operations: 16.6 us -> 0.65 us
  other arithmetic: 10.8 us -> 0 us
    psum x2 -> x0, waiting for transfers between devices: 470 us -> none  [local(): summed = lax.psum(terms, ('row', 'col'))]
    pallas_call x0 -> x1, Pallas kernels: none -> 110 us  [local(): pl.pallas_call(kernel, out_shape=(jax.ShapeDtypeStruct((2, TILE, TILE), F...]
    dot_general x36 -> x0, matrix products: 83.8 us -> none  [the longest x16 34.9 us: right_apply(): jnp.einsum('bjk,kl->bjl', fields, matrix, precision=lax.Precision.HIGHEST)]
    gather x96 -> x0, local copies, waits for them, and re-layouts: 81.1 us -> none
    ppermute x16 -> x0, starting transfers between devices: 58.9 us -> none  [the longest x8 28 us: passed_along(): lax.ppermute(value, axis, [(source, source + steps) for source in range(l...]
    ppermute x16 -> x0, waiting for transfers between devices: 35.3 us -> none  [the longest x4 19.9 us: padded_2(): after = lax.ppermute(leading, axis, down)]
  transfers between devices with their start and end apart: 18 -> 0, of which waited for: 12 -> 0; matrix products, arithmetic and copies ran while one was open for 3% -> 0% of each run, Pallas kernels for 0% -> 0%
where the time goes in v1:
time: 119 us; the launch traced here: 118 us
  Pallas kernels  110 us (92%)
  local copies, waits for them, and re-layouts  7.38 us (6%)
    pallas_call x1, Pallas kernels, local(): pl.pallas_call(kernel, out_shape=(jax.ShapeDtypeStruct((2, TILE, TILE), F...  110 us
    unnamed x14, local copies, waits for them, and re-layouts  7.38 us

profile of v1, /device:TPU:1, one launch (start us, length us, event | category | flops | bytes accessed | tf_op | source)
XLA Modules:
  0.0 118.5 jit_solution(1481679158324176707)
XLA Ops:
  0.6 0.0 copy-start
  0.6 1.6 %copy-done = f32[2,1,1,16,128,128]{5,4,3,2,1,0:T(8,128)S(1)} copy-done((f32[2,1,1,16,128,128]{5,4,3,2,1,0:T(8,128)S(1)}, f32[2,1,1,16,128,128]{5,4,3,2,1,0:T(8,128)}, u32[]{:S(2)}) %copy-start) | copy-done | bytes 2097176
  2.2 0.0 copy-start.1
  2.2 1.0 copy-done.1
  3.3 0.0 copy-start.2
  3.3 1.0 copy-done.2
  4.3 0.0 copy-start.3
  4.3 0.9 copy-done.3
  5.2 0.0 copy-start.4
  5.2 0.7 copy-done.4
  5.9 0.0 copy-start.5
  5.9 0.7 copy-done.5
  6.6 110.5 %shard_map.77 = (f32[2,256,256]{2,1,0:T(8,128)S(1)}, f32[2,128,128]{2,1,0:T(8,128)S(1)}) custom-call(f32[2,256,256]{2,1,0:T(8,128)S(1)} %copy-done.1, f32[2,128,128]{2,1,0:T(8,128)S(1)} %copy-done.3, f32[2,1,1,16,128,128]{5,4,3,2,1,0:T(8,128)S(1)} %copy-done, s32[2,2,1,1,16]{4,3,2,1,0:T(1,128)S(1)} %copy-done.4, s32[2,2,1,1,16]{4,3,2,1,0:T(1,128)S(1)} %copy-done.5, ...), custom_call_target="tpu_custom_call" | custom-call | tf_op jit(solution)/shard_map/pallas_call | solution.py:470
  117.0 0.8 copy.10
  117.8 0.7 copy.11
Async XLA Ops:
  0.6 1.6 %copy-start = (f32[2,1,1,16,128,128]{5,4,3,2,1,0:T(8,128)S(1)}, f32[2,1,1,16,128,128]{5,4,3,2,1,0:T(8,128)}, u32[]{:S(2)}) copy-start(f32[2,1,1,16,128,128]{5,4,3,2,1,0:T(8,128)} %amp_in.1) | copy-start | bytes 6291460
  2.2 1.0 copy-start.1
  3.3 1.0 copy-start.2
  4.3 0.9 copy-start.3
  5.2 0.7 copy-start.4
  5.9 0.7 copy-start.5

commit v2 on v1

v2 whole, which is shorter than its diff:
```python
import functools
import math

import jax
import jax.numpy as jnp
import numpy as np
from jax import lax
from jax.experimental import pallas as pl
from jax.experimental.pallas import tpu as pltpu
from jax.sharding import PartitionSpec as P

MESH = pl.DeviceIdType.MESH
F32 = jnp.float32
BF16 = jnp.bfloat16

WIDTH = 128
HALF = 64
TILE = 256
PAD = TILE + 2 * HALF
BLOCKS = 4
BATCH = 16
ITERS = 2
N_ROW = 16
N_COL = 16
NX, NY, NZ = 4, 4, 8
PATTERNS = BATCH * N_ROW * N_COL
TERM_ROWS = 3 * WIDTH
CHUNK = TERM_ROWS // (NX * NY)
CENTRE = 256
PLACED = CENTRE + WIDTH + 256


def tables():
    n = np.arange(WIDTH)
    angle = (np.outer(n, n) % WIDTH) * (2.0 * math.pi / WIDTH)
    c, s = np.cos(angle) / math.sqrt(WIDTH), np.sin(angle) / math.sqrt(WIDTH)
    return np.stack([np.block([[c, s], [-s, c]]), np.block([[c, -s], [s, c]])]).astype(np.float32)


def split(x):
    high = x.astype(BF16)
    return high, (x - high.astype(F32)).astype(BF16)


def mm(a, b):
    return jnp.dot(a, b, preferred_element_type=F32)


def left_mul(high, low, x):
    xh, xl = split(x)
    return mm(high, xh) + mm(high, xl) + mm(low, xh)


def right_mul(x, high, low):
    xh, xl = split(x)
    return mm(xh, high) + mm(xl, high) + mm(xh, low)


def swap_quadrants(y):
    top = jnp.concatenate([y[:WIDTH, :WIDTH], y[WIDTH:, :WIDTH]], axis=1)
    low = jnp.concatenate([y[:WIDTH, WIDTH:], y[WIDTH:, WIDTH:]], axis=1)
    return jnp.concatenate([top, low], axis=0)


def kernel(
    obj_in, probe_in, amp_in, pos_in, shf_in, tab_in, new_obj, new_probe,
    pos, shf, tab32, tab, obj, prb, amp, zb, grad, terms, pack, fold_row, fold_col, fold_cor,
    hpack, hbuf, xy_buf, zc_buf, summed,
    in_sem, halo_s, halo_r, fold_s, fold_r, xy_s, xy_r, zc_s, zc_r, out_s, out_r,
):
    r, c = lax.axis_index("row"), lax.axis_index("col")
    y, zh, core = r // 4, (r // 2) % 2, r % 2
    zl, x = c // 4, c % 4
    zc = (zh * 4 + zl) * 2 + core
    xy = y * NX + x

    def near(dr, dc):
        return ((r + dr + N_ROW) % N_ROW, (c + dc + N_COL) % N_COL)

    def at_zc(d):
        other = (zc + d) % (2 * NZ)
        return (y * 4 + (other // 8) * 2 + other % 2, ((other // 2) % 4) * 4 + x)

    def at_xy(d):
        other = (xy + d) % (NX * NY)
        return ((other // NX) * 4 + zh * 2 + core, zl * 4 + other % NX)

    around = [(-1, 0), (1, 0), (0, -1), (0, 1), (-1, -1), (-1, 1), (1, -1), (1, 1), (-1, 0), (1, 0)]

    barrier = pltpu.get_barrier_semaphore()
    peers = [near(*d) for d in around[:8]]
    peers += [at_zc(d) for d in range(1, 2 * NZ)] + [at_xy(d) for d in range(1, NX * NY)]
    for peer in peers:
        pl.semaphore_signal(barrier, inc=1, device_id=peer, device_id_type=MESH)

    loads = [
        pltpu.make_async_copy(obj_in.at[:, :, 0:128], obj.at[:, 1, HALF:HALF + TILE], in_sem.at[0]),
        pltpu.make_async_copy(obj_in.at[:, :, 128:256], obj.at[:, 2, HALF:HALF + TILE], in_sem.at[1]),
        pltpu.make_async_copy(probe_in, prb, in_sem.at[2]),
        pltpu.make_async_copy(pos_in, pos, in_sem.at[3]),
        pltpu.make_async_copy(shf_in, shf, in_sem.at[4]),
        pltpu.make_async_copy(tab_in, tab32, in_sem.at[5]),
        pltpu.make_async_copy(amp_in.at[:, 0, 0], amp, in_sem.at[6]),
    ]
    for load in loads:
        load.start()

    lane = lax.broadcasted_iota(jnp.int32, (HALF, WIDTH), 1)
    lane_full = lax.broadcasted_iota(jnp.int32, (WIDTH, WIDTH), 1)
    low_half = lane < HALF

    def remote(src, dst, ss, rs, to):
        return pltpu.make_async_remote_copy(
            src_ref=src, dst_ref=dst, send_sem=ss, recv_sem=rs, device_id=to, device_id_type=MESH
        )

    def halo_copies(h):
        src = [
            obj.at[:, 1, 64:128], obj.at[:, 1, 256:320], hpack.at[h, 0], hpack.at[h, 1],
            hpack.at[h, 0, 0:64], hpack.at[h, 1, 0:64], hpack.at[h, 0, 192:256], hpack.at[h, 1, 192:256],
            obj.at[:, 2, 64:128], obj.at[:, 2, 256:320],
        ]
        dst = [
            obj.at[:, 1, 320:384], obj.at[:, 1, 0:64], hbuf.at[h, 0, 64:320], hbuf.at[h, 1, 64:320],
            hbuf.at[h, 0, 320:384], hbuf.at[h, 1, 320:384], hbuf.at[h, 0, 0:64], hbuf.at[h, 1, 0:64],
            obj.at[:, 2, 320:384], obj.at[:, 2, 0:64],
        ]
        return [
            remote(src[i], dst[i], halo_s.at[h, i], halo_r.at[h, i], near(*around[i])) for i in range(10)
        ]

    def halo_send(h, copies, j):
        for t in (0, 3, 1, 2):
            rows = slice(HALF + 64 * t, HALF + 64 * t + 64)
            to = slice(64 * t, 64 * t + 64)
            re, im = obj[0, j, rows], obj[1, j, rows]
            if j == 1:
                hpack[h, 0, to] = jnp.where(low_half, re, pltpu.roll(im, 64, 1))
            else:
                hpack[h, 1, to] = jnp.where(low_half, pltpu.roll(re, 64, 1), im)
            if t == 3:
                for i in (4, 6, 0, 1) if j == 1 else (5, 7, 8, 9):
                    copies[i].start()
        copies[2 if j == 1 else 3].start()

    def halo_finish(h, copies):
        for copy in copies:
            copy.wait()
        for t in range(6):
            rows = slice(64 * t, 64 * t + 64)
            inside = r >= 0
            if t == 0:
                inside = r > 0
            if t == 5:
                inside = r < N_ROW - 1
            right = jnp.where(jnp.logical_and(inside, c < N_COL - 1), hbuf[h, 0, rows], 0.0)
            left = jnp.where(jnp.logical_and(inside, c > 0), hbuf[h, 1, rows], 0.0)
            obj[0, 3, rows] = right
            obj[1, 3, rows] = pltpu.roll(right, 64, 1)
            obj[0, 0, rows] = pltpu.roll(left, 64, 1)
            obj[1, 0, rows] = left

        @pl.when(r == 0)
        def _():
            obj[:, 1:3, 0:64] = jnp.zeros((2, 2, 64, WIDTH), F32)

        @pl.when(r == N_ROW - 1)
        def _():
            obj[:, 1:3, 320:384] = jnp.zeros((2, 2, 64, WIDTH), F32)

    def place_of(it, b):
        u = lax.bitwise_and(pos[0, it, 0, 0, b] + shf[0, it, 0, 0, b], TILE - 1)
        w = lax.bitwise_and(pos[1, it, 0, 0, b] + shf[1, it, 0, 0, b], TILE - 1) + HALF
        return u, lax.shift_right_arithmetic(w, 7), lax.bitwise_and(w, 127)

    def patterns(it, first, count):
        pr, pi = prb[0], prb[1]
        ah, al, bh, bl = tab[0], tab[1], tab[2], tab[3]
        patches, shifts_of, stage = [], [], []
        weight = terms[256:384]
        for p in range(count):
            fields = []
            for i in range(2):
                u, k, s = place_of(it, first + 2 * p + i)
                window = lane_full >= s
                parts = []
                for part in range(2):
                    near_block = obj[part, k, pl.ds(u, WIDTH), :]
                    next_block = obj[part, k + 1, pl.ds(u, WIDTH), :]
                    back_by = lax.bitwise_and(WIDTH - s, 127)
                    parts.append(pltpu.roll(jnp.where(window, near_block, next_block), back_by, 1))
                o_re, o_im = parts
                weight = weight + (o_re * o_re + o_im * o_im)
                patches.append((o_re, o_im))
                shifts_of.append(s)
                fields.append((pr * o_re - pi * o_im, pr * o_im + pi * o_re))
            stage.append(
                jnp.concatenate(
                    [
                        jnp.concatenate([fields[0][0], fields[1][0]], axis=1),
                        jnp.concatenate([fields[0][1], fields[1][1]], axis=1),
                    ],
                    axis=0,
                )
            )
        terms[256:384] = weight
        stage = [left_mul(ah, al, v) for v in stage]
        stage = [right_mul(swap_quadrants(v), bh, bl) for v in stage]
        kept = []
        for p, v in enumerate(stage):
            f_re, f_im = v[:, :WIDTH], v[:, WIDTH:]
            measured = amp[it, pl.ds(first + 2 * p, 2)].reshape(2 * WIDTH, WIDTH)
            keep = 1.0 - measured * lax.rsqrt(jnp.maximum(f_re * f_re + f_im * f_im, 1.0))
            kept.append(jnp.concatenate([keep * f_re, keep * f_im], axis=1))
        stage = [right_mul(v, ah, al) for v in kept]
        stage = [left_mul(bh, bl, swap_quadrants(v)) for v in stage]
        q_re, q_im = terms[0:128], terms[128:256]
        for p, v in enumerate(stage):
            for i in range(2):
                b_re = v[:WIDTH, i * WIDTH:(i + 1) * WIDTH]
                b_im = v[WIDTH:, i * WIDTH:(i + 1) * WIDTH]
                o_re, o_im = patches[2 * p + i]
                q_re = q_re + (o_re * b_re + o_im * b_im)
                q_im = q_im + (o_re * b_im - o_im * b_re)
                s = shifts_of[2 * p + i]
                b = first + 2 * p + i
                zb[b, 0, CENTRE:CENTRE + WIDTH] = pltpu.roll(pr * b_re + pi * b_im, s, 1)
                zb[b, 1, CENTRE:CENTRE + WIDTH] = pltpu.roll(pr * b_im - pi * b_re, s, 1)
        terms[0:128] = q_re
        terms[128:256] = q_im

    def gather_gradient(it, j, t):
        def add(b, acc):
            u, k, s = place_of(it, b)
            start = CENTRE - u + 64 * t
            low = jnp.where(k == j, s, WIDTH)
            high = jnp.where(k + 1 == j, s, 0)
            mine = jnp.logical_or(lane >= low, lane < high)
            return tuple(
                acc[part] + jnp.where(mine, zb[b, part, pl.ds(start, 64), :], 0.0) for part in range(2)
            )

        zero = jnp.zeros((64, WIDTH), F32)
        re, im = lax.fori_loop(0, BATCH, add, (zero, zero), unroll=4)
        if isinstance(t, int):
            rows = slice(64 * t, 64 * t + 64)
        else:
            rows = pl.ds(pl.multiple_of(64 * t, 64), 64)
        grad[0, j, rows] = re
        grad[1, j, rows] = im
        return re, im

    def fold_copies(it):
        src = [
            grad.at[:, 1, 0:64], grad.at[:, 1, 320:384], pack.at[0, 64:320], pack.at[1, 64:320],
            pack.at[0, 0:64], pack.at[1, 0:64], pack.at[0, 320:384], pack.at[1, 320:384],
            grad.at[:, 2, 0:64], grad.at[:, 2, 320:384],
        ]
        dst = [
            fold_row.at[0, 0], fold_row.at[1, 0], fold_col.at[0], fold_col.at[1],
            fold_cor.at[0], fold_cor.at[1], fold_cor.at[2], fold_cor.at[3],
            fold_row.at[0, 1], fold_row.at[1, 1],
        ]
        return [
            remote(src[i], dst[i], fold_s.at[it, i], fold_r.at[it, i], near(*around[i])) for i in range(10)
        ]

    def rim(it, t):
        re, im = gather_gradient(it, 0, t)
        rows = slice(64 * t, 64 * t + 64) if isinstance(t, int) else pl.ds(pl.multiple_of(64 * t, 64), 64)
        pack[0, rows] = jnp.where(low_half, pltpu.roll(re, 64, 1), im)
        re, im = gather_gradient(it, 3, t)
        pack[1, rows] = jnp.where(low_half, re, pltpu.roll(im, 64, 1))

    def fold_send(it):
        copies = fold_copies(it)
        for t, corners in ((0, (4, 5)), (5, (6, 7))):
            rim(it, t)
            for i in corners:
                copies[i].start()
        for j in (1, 2):
            for t in (0, 5):
                gather_gradient(it, j, t)
                copies[(0 if j == 1 else 8) + t // 5].start()

        def middle(t, carry):
            rim(it, t)
            return carry

        lax.fori_loop(1, 5, middle, 0)
        copies[2].start()
        copies[3].start()
        return copies

    def interior(it):
        def rows(t, carry):
            gather_gradient(it, 1, t)
            gather_gradient(it, 2, t)
            return carry

        lax.fori_loop(1, 5, rows, 0)

    def fold_finish(copies, step, j):
        for i in (0, 1, 3, 5, 7) if j == 1 else (8, 9, 2, 4, 6):
            copies[i].wait()
        up, down = r > 0, r < N_ROW - 1
        beside = c > 0 if j == 1 else c < N_COL - 1
        for t in range(4):
            rows = slice(HALF + 64 * t, HALF + 64 * t + 64)
            at = slice(64 * t, 64 * t + 64)
            side = jnp.where(beside, fold_col[2 - j if j == 2 else 1, at], 0.0)
            if t == 0:
                side = side + jnp.where(jnp.logical_and(up, beside), fold_cor[3 if j == 1 else 2], 0.0)
            if t == 3:
                side = side + jnp.where(jnp.logical_and(down, beside), fold_cor[1 if j == 1 else 0], 0.0)
            if j == 1:
                added = [jnp.where(low_half, side, 0.0), jnp.where(low_half, pltpu.roll(side, 64, 1), 0.0)]
            else:
                added = [jnp.where(low_half, 0.0, pltpu.roll(side, 64, 1)), jnp.where(low_half, 0.0, side)]
            for part in range(2):
                g = grad[part, j, rows] + added[part]
                if t == 0:
                    g = g + jnp.where(up, fold_row[1, j - 1, part], 0.0)
                if t == 3:
                    g = g + jnp.where(down, fold_row[0, j - 1, part], 0.0)
                obj[part, j, rows] = obj[part, j, rows] - step * g

    def chunk(i):
        return pl.ds(pl.multiple_of(i * CHUNK, 8), CHUNK)

    def xy_scatter(it):
        copies = []
        for d in range(1, NX * NY):
            copies.append(
                remote(
                    terms.at[chunk((xy + d) % (NX * NY))], xy_buf.at[it, d],
                    xy_s.at[it, d], xy_r.at[it, d], at_xy(d),
                )
            )
            copies[-1].start()
        return copies

    def zc_gather(it, before):
        for copy in before:
            copy.wait()
        value = terms[chunk(xy)]
        for d in range(1, NX * NY):
            value = value + xy_buf[it, d]
        zc_buf[it, zc] = value
        for d in range(1, 2 * NZ):
            remote(zc_buf.at[it, zc], zc_buf.at[it, zc], zc_s.at[it, d], zc_r.at[it, d], at_zc(d)).start()

    def xy_gather(it):
        for d in range(1, 2 * NZ):
            arriving = zc_buf.at[it, (zc + 2 * NZ - d) % (2 * NZ)]
            remote(zc_buf.at[it, zc], arriving, zc_s.at[it, d], zc_r.at[it, d], at_zc(d)).wait()
        value = zc_buf[it, 0]
        for d in range(1, 2 * NZ):
            value = value + zc_buf[it, d]
        summed[it, chunk(xy)] = value
        rows = summed.at[it, chunk(xy)]
        for d in range(1, NX * NY):
            remote(rows, rows, out_s.at[it, d], out_r.at[it, d], at_xy(d)).start()

    def new_probe_from(it):
        rows = summed.at[it, chunk(xy)]
        for d in range(1, NX * NY):
            arriving = summed.at[it, chunk((xy + NX * NY - d) % (NX * NY))]
            remote(rows, arriving, out_s.at[it, d], out_r.at[it, d], at_xy(d)).wait()
        under = summed[it, 256:384] + 0.2 * PATTERNS
        prb[0] = prb[0] - summed[it, 0:128] / under
        prb[1] = prb[1] - summed[it, 128:256] / under

    loads[0].wait()
    loads[1].wait()
    pl.semaphore_wait(barrier, len(peers))
    copies = halo_copies(0)
    halo_send(0, copies, 1)
    halo_send(0, copies, 2)

    def clear(b, carry):
        for part in range(2):
            zb[b, part, 0:CENTRE] = jnp.zeros((CENTRE, WIDTH), F32)
            zb[b, part, CENTRE + WIDTH:] = jnp.zeros((PLACED - CENTRE - WIDTH, WIDTH), F32)
        return carry

    lax.fori_loop(0, BATCH, clear, 0)
    for load in loads[2:]:
        load.wait()
    for m in range(2):
        tab[2 * m], tab[2 * m + 1] = split(tab32[m])
    halo_finish(0, copies)

    for it in range(ITERS):
        terms[...] = jnp.zeros((TERM_ROWS, WIDTH), F32)

        def some(g, carry):
            patterns(it, g * 4, 2)
            return carry

        lax.fori_loop(0, BATCH // 4, some, 0)
        power = prb[0] * prb[0] + prb[1] * prb[1]
        step = 0.5 / (jnp.max(power) + 1e-6)
        summing = xy_scatter(it)
        folds = fold_send(it)
        interior(it)
        zc_gather(it, summing)
        if it + 1 < ITERS:
            copies = halo_copies(it + 1)
        else:
            stores = [
                pltpu.make_async_copy(
                    obj.at[:, 1 + j, HALF:HALF + TILE], new_obj.at[:, :, j * 128:(j + 1) * 128], in_sem.at[7 + j]
                )
                for j in range(2)
            ]
        for j in (1, 2):
            fold_finish(folds, step, j)
            if it + 1 < ITERS:
                halo_send(it + 1, copies, j)
            else:
                stores[j - 1].start()
        xy_gather(it)
        new_probe_from(it)
        if it + 1 < ITERS:
            halo_finish(it + 1, copies)
    stores.append(pltpu.make_async_copy(prb, new_probe, in_sem.at[9]))
    stores[2].start()
    for store in stores:
        store.wait()


def local(object_field, probe_field, amplitudes, positions, shifts):
    hbm = pl.BlockSpec(memory_space=pltpu.HBM)
    dma = pltpu.SemaphoreType.DMA
    scratch = [
        pltpu.SMEM(positions.shape, jnp.int32),
        pltpu.SMEM(shifts.shape, jnp.int32),
        pltpu.VMEM((2, 2 * WIDTH, 2 * WIDTH), F32),
        pltpu.VMEM((4, 2 * WIDTH, 2 * WIDTH), BF16),
        pltpu.VMEM((2, BLOCKS, PAD, WIDTH), F32),
        pltpu.VMEM((2, WIDTH, WIDTH), F32),
        pltpu.VMEM((ITERS, BATCH, WIDTH, WIDTH), F32),
        pltpu.VMEM((BATCH, 2, PLACED, WIDTH), F32),
        pltpu.VMEM((2, BLOCKS, PAD, WIDTH), F32),
        pltpu.VMEM((TERM_ROWS, WIDTH), F32),
        pltpu.VMEM((2, PAD, WIDTH), F32),
        pltpu.VMEM((2, 2, 2, HALF, WIDTH), F32),
        pltpu.VMEM((2, TILE, WIDTH), F32),
        pltpu.VMEM((4, HALF, WIDTH), F32),
        pltpu.VMEM((ITERS, 2, TILE, WIDTH), F32),
        pltpu.VMEM((ITERS, 2, PAD, WIDTH), F32),
        pltpu.VMEM((ITERS, NX * NY, CHUNK, WIDTH), F32),
        pltpu.VMEM((ITERS, 2 * NZ, CHUNK, WIDTH), F32),
        pltpu.VMEM((ITERS, TERM_ROWS, WIDTH), F32),
        dma((10,)),
        dma((ITERS, 10)), dma((ITERS, 10)),
        dma((ITERS, 10)), dma((ITERS, 10)),
        dma((ITERS, NX * NY)), dma((ITERS, NX * NY)),
        dma((ITERS, 2 * NZ)), dma((ITERS, 2 * NZ)),
        dma((ITERS, NX * NY)), dma((ITERS, NX * NY)),
    ]
    return pl.pallas_call(
        kernel,
        out_shape=(
            jax.ShapeDtypeStruct((2, TILE, TILE), F32),
            jax.ShapeDtypeStruct((2, WIDTH, WIDTH), F32),
        ),
        in_specs=[hbm] * 6,
        out_specs=(hbm, hbm),
        scratch_shapes=scratch,
        compiler_params=pltpu.CompilerParams(
            collective_id=0, has_side_effects=True, vmem_limit_bytes=60 * 1024 * 1024
        ),
    )(object_field, probe_field, amplitudes, positions, shifts, jnp.asarray(tables()))


def solution(mesh):
    in_specs = (
        P(None, "row", "col"),
        P(),
        P(None, "row", "col", None, None, None),
        P(None, None, "row", "col", None),
        P(None, None, "row", "col", None),
    )
    out_specs = (P(None, "row", "col"), P())
    return jax.shard_map(local, mesh=mesh, in_specs=in_specs, out_specs=out_specs, check_vma=False)
```

time: 119 us -> 102 us (0.86)
  Pallas kernels: 110 us -> 97.8 us
  local copies, waits for them, and re-layouts: 7.38 us -> 3.44 us
    pallas_call x1, Pallas kernels: 110 us -> 97.8 us  [local(): pl.pallas_call(kernel, out_shape=(jax.ShapeDtypeStruct((2, TILE, TILE), F...]
    unnamed x14 -> x2, local copies, waits for them, and re-layouts: 7.38 us -> 3.44 us
where the time goes in v2:
time: 102 us
  Pallas kernels  97.8 us (96%)
  local copies, waits for them, and re-layouts  3.44 us (3%)
    pallas_call x1, Pallas kernels, local(): pl.pallas_call(kernel, out_shape=(jax.ShapeDtypeStruct((2, TILE, TILE), F...  97.8 us
    unnamed x2, local copies, waits for them, and re-layouts  3.44 us

profile of v2, /device:TPU:1, one launch (start us, length us, event | category | flops | bytes accessed | tf_op | source)
XLA Modules:
  0.0 101.8 jit_solution(9449485842163137385)
XLA Ops:
  0.6 97.8 %shard_map.77 = (f32[2,256,256]{2,1,0:T(8,128)}, f32[2,128,128]{2,1,0:T(8,128)}) custom-call(f32[2,256,256]{2,1,0:T(8,128)} %obj_in.1, f32[2,128,128]{2,1,0:T(8,128)} %probe_in.1, f32[2,1,1,16,128,128]{5,4,3,2,1,0:T(8,128)} %amp_in.1, s32[2,2,1,1,16]{4,3,2,1,0:T(1,128)} %pos_in.1, s32[2,2,1,1,16]{4,3,2,1,0:T(1,128)} %shf_in.1, ...), custom_call_target="tpu_custom_call" | custom-call | tf_op jit(solution)/shard_map/pallas_call | solution.py:463
  98.4 1.9 %copy.10 = f32[2,256,256]{2,1,0:T(8,128)} copy(f32[2,256,256]{2,1,0:T(8,128)} %get-tuple-element.4) | data formatting | bytes 1048576
  100.3 1.6 %copy.11 = f32[2,128,128]{2,1,0:T(8,128)} copy(f32[2,128,128]{2,1,0:T(8,128)} %get-tuple-element.5) | data formatting | bytes 262144

commit v3 on v2

--- a/solution.py
+++ b/solution.py
@@ -65,31 +65,32 @@
 def kernel(
     obj_in, probe_in, amp_in, pos_in, shf_in, tab_in, new_obj, new_probe,
     pos, shf, tab32, tab, obj, prb, amp, zb, grad, terms, pack, fold_row, fold_col, fold_cor,
-    hpack, hbuf, xy_buf, zc_buf, summed,
-    in_sem, halo_s, halo_r, fold_s, fold_r, xy_s, xy_r, zc_s, zc_r, out_s, out_r,
+    hpack, hbuf, xy_buf, pair_buf, z_buf, summed,
+    in_sem, halo_s, halo_r, fold_s, fold_r, xy_s, xy_r, pair_s, pair_r, z_s, z_r, out_s, out_r,
 ):
     r, c = lax.axis_index("row"), lax.axis_index("col")
     y, zh, core = r // 4, (r // 2) % 2, r % 2
     zl, x = c // 4, c % 4
-    zc = (zh * 4 + zl) * 2 + core
+    z = zh * 4 + zl
     xy = y * NX + x
 
     def near(dr, dc):
         return ((r + dr + N_ROW) % N_ROW, (c + dc + N_COL) % N_COL)
 
-    def at_zc(d):
-        other = (zc + d) % (2 * NZ)
-        return (y * 4 + (other // 8) * 2 + other % 2, ((other // 2) % 4) * 4 + x)
+    def at_z(d):
+        other = (z + d) % NZ
+        return (y * 4 + (other // 4) * 2 + core, (other % 4) * 4 + x)
 
     def at_xy(d):
         other = (xy + d) % (NX * NY)
         return ((other // NX) * 4 + zh * 2 + core, zl * 4 + other % NX)
 
+    partner = (r + 1 - 2 * core, c)
     around = [(-1, 0), (1, 0), (0, -1), (0, 1), (-1, -1), (-1, 1), (1, -1), (1, 1), (-1, 0), (1, 0)]
 
     barrier = pltpu.get_barrier_semaphore()
     peers = [near(*d) for d in around[:8]]
-    peers += [at_zc(d) for d in range(1, 2 * NZ)] + [at_xy(d) for d in range(1, NX * NY)]
+    peers += [partner] + [at_z(d) for d in range(1, NZ)] + [at_xy(d) for d in range(1, NX * NY)]
     for peer in peers:
         pl.semaphore_signal(barrier, inc=1, device_id=peer, device_id_type=MESH)
 
@@ -113,6 +114,30 @@
         return pltpu.make_async_remote_copy(
             src_ref=src, dst_ref=dst, send_sem=ss, recv_sem=rs, device_id=to, device_id_type=MESH
         )
+
+    def inside(dr, dc):
+        has = [r > 0] if dr < 0 else [r < N_ROW - 1] if dr > 0 else []
+        has += [c > 0] if dc < 0 else [c < N_COL - 1] if dc > 0 else []
+        return has[0] if len(has) == 1 else jnp.logical_and(*has)
+
+    def start(copies, which):
+        for i in which:
+
+            @pl.when(inside(*around[i]))
+            def _(copy=copies[i]):
+                copy.start()
+
+    def finish(copies, which):
+        for i in which:
+            dr, dc = around[i]
+
+            @pl.when(inside(dr, dc))
+            def _(copy=copies[i]):
+                copy.wait_send()
+
+            @pl.when(inside(-dr, -dc))
+            def _(copy=copies[i]):
+                copy.wait_recv()
 
     def halo_copies(h):
         src = [
@@ -139,22 +164,16 @@
             else:
                 hpack[h, 1, to] = jnp.where(low_half, pltpu.roll(re, 64, 1), im)
             if t == 3:
-                for i in (4, 6, 0, 1) if j == 1 else (5, 7, 8, 9):
-                    copies[i].start()
-        copies[2 if j == 1 else 3].start()
+                start(copies, (4, 6, 0, 1) if j == 1 else (5, 7, 8, 9))
+        start(copies, (2,) if j == 1 else (3,))
 
     def halo_finish(h, copies):
-        for copy in copies:
-            copy.wait()
+        finish(copies, range(10))
         for t in range(6):
             rows = slice(64 * t, 64 * t + 64)
-            inside = r >= 0
-            if t == 0:
-                inside = r > 0
-            if t == 5:
-                inside = r < N_ROW - 1
-            right = jnp.where(jnp.logical_and(inside, c < N_COL - 1), hbuf[h, 0, rows], 0.0)
-            left = jnp.where(jnp.logical_and(inside, c > 0), hbuf[h, 1, rows], 0.0)
+            dr = -1 if t == 0 else 1 if t == 5 else 0
+            right = jnp.where(inside(dr, 1), hbuf[h, 0, rows], 0.0)
+            left = jnp.where(inside(dr, -1), hbuf[h, 1, rows], 0.0)
             obj[0, 3, rows] = right
             obj[1, 3, rows] = pltpu.roll(right, 64, 1)
             obj[0, 0, rows] = pltpu.roll(left, 64, 1)
@@ -276,20 +295,19 @@
         copies = fold_copies(it)
         for t, corners in ((0, (4, 5)), (5, (6, 7))):
             rim(it, t)
-            for i in corners:
-                copies[i].start()
+            start(copies, corners)
         for j in (1, 2):
             for t in (0, 5):
                 gather_gradient(it, j, t)
-                copies[(0 if j == 1 else 8) + t // 5].start()
+                start(copies, [(0 if j == 1 else 8) + t // 5])
 
         def middle(t, carry):
             rim(it, t)
             return carry
 
         lax.fori_loop(1, 5, middle, 0)
-        copies[2].start()
-        copies[3].start()
+        if it + 1 < ITERS:
+            start(copies, (2, 3))
         return copies
 
     def interior(it):
@@ -301,10 +319,9 @@
         lax.fori_loop(1, 5, rows, 0)
 
     def fold_finish(copies, step, j):
-        for i in (0, 1, 3, 5, 7) if j == 1 else (8, 9, 2, 4, 6):
-            copies[i].wait()
-        up, down = r > 0, r < N_ROW - 1
-        beside = c > 0 if j == 1 else c < N_COL - 1
+        finish(copies, (0, 1, 3, 5, 7) if j == 1 else (8, 9, 2, 4, 6))
+        up, down = inside(-1, 0), inside(1, 0)
+        beside = inside(0, -1 if j == 1 else 1)
         for t in range(4):
             rows = slice(HALF + 64 * t, HALF + 64 * t + 64)
             at = slice(64 * t, 64 * t + 64)
@@ -340,23 +357,27 @@
             copies[-1].start()
         return copies
 
-    def zc_gather(it, before):
+    def z_gather(it, before):
         for copy in before:
             copy.wait()
         value = terms[chunk(xy)]
         for d in range(1, NX * NY):
             value = value + xy_buf[it, d]
-        zc_buf[it, zc] = value
-        for d in range(1, 2 * NZ):
-            remote(zc_buf.at[it, zc], zc_buf.at[it, zc], zc_s.at[it, d], zc_r.at[it, d], at_zc(d)).start()
+        pair_buf[it, 0] = value
+        swap = remote(pair_buf.at[it, 0], pair_buf.at[it, 1], pair_s.at[it], pair_r.at[it], partner)
+        swap.start()
+        swap.wait()
+        z_buf[it, z] = value + pair_buf[it, 1]
+        for d in range(1, NZ):
+            remote(z_buf.at[it, z], z_buf.at[it, z], z_s.at[it, d], z_r.at[it, d], at_z(d)).start()
 
     def xy_gather(it):
-        for d in range(1, 2 * NZ):
-            arriving = zc_buf.at[it, (zc + 2 * NZ - d) % (2 * NZ)]
-            remote(zc_buf.at[it, zc], arriving, zc_s.at[it, d], zc_r.at[it, d], at_zc(d)).wait()
-        value = zc_buf[it, 0]
-        for d in range(1, 2 * NZ):
-            value = value + zc_buf[it, d]
+        for d in range(1, NZ):
+            arriving = z_buf.at[it, (z + NZ - d) % NZ]
+            remote(z_buf.at[it, z], arriving, z_s.at[it, d], z_r.at[it, d], at_z(d)).wait()
+        value = z_buf[it, 0]
+        for d in range(1, NZ):
+            value = value + z_buf[it, d]
         summed[it, chunk(xy)] = value
         rows = summed.at[it, chunk(xy)]
         for d in range(1, NX * NY):
@@ -395,16 +416,18 @@
         terms[...] = jnp.zeros((TERM_ROWS, WIDTH), F32)
 
         def some(g, carry):
-            patterns(it, g * 4, 2)
+            patterns(it, g * 8, 4)
             return carry
 
-        lax.fori_loop(0, BATCH // 4, some, 0)
+        lax.fori_loop(0, BATCH // 8, some, 0)
         power = prb[0] * prb[0] + prb[1] * prb[1]
         step = 0.5 / (jnp.max(power) + 1e-6)
         summing = xy_scatter(it)
         folds = fold_send(it)
         interior(it)
-        zc_gather(it, summing)
+        z_gather(it, summing)
+        if it + 1 == ITERS:
+            start(folds, (2, 3))
         if it + 1 < ITERS:
             copies = halo_copies(it + 1)
         else:
@@ -451,13 +474,15 @@
         pltpu.VMEM((ITERS, 2, TILE, WIDTH), F32),
         pltpu.VMEM((ITERS, 2, PAD, WIDTH), F32),
         pltpu.VMEM((ITERS, NX * NY, CHUNK, WIDTH), F32),
-        pltpu.VMEM((ITERS, 2 * NZ, CHUNK, WIDTH), F32),
+        pltpu.VMEM((ITERS, 2, CHUNK, WIDTH), F32),
+        pltpu.VMEM((ITERS, NZ, CHUNK, WIDTH), F32),
         pltpu.VMEM((ITERS, TERM_ROWS, WIDTH), F32),
         dma((10,)),
         dma((ITERS, 10)), dma((ITERS, 10)),
         dma((ITERS, 10)), dma((ITERS, 10)),
         dma((ITERS, NX * NY)), dma((ITERS, NX * NY)),
-        dma((ITERS, 2 * NZ)), dma((ITERS, 2 * NZ)),
+        dma((ITERS,)), dma((ITERS,)),
+        dma((ITERS, NZ)), dma((ITERS, NZ)),
         dma((ITERS, NX * NY)), dma((ITERS, NX * NY)),
     ]
     return pl.pallas_call(

time: 102 us -> 91.9 us (0.901)
  Pallas kernels: 97.8 us -> 87.7 us
    pallas_call x1, Pallas kernels: 97.8 us -> 87.7 us  [local(): pl.pallas_call(kernel, out_shape=(jax.ShapeDtypeStruct((2, TILE, TILE), F...]
where the time goes in v3:
time: 91.9 us; the launch traced here: 91.8 us
  Pallas kernels  87.7 us (95%)
  local copies, waits for them, and re-layouts  3.44 us (4%)
    pallas_call x1, Pallas kernels, local(): pl.pallas_call(kernel, out_shape=(jax.ShapeDtypeStruct((2, TILE, TILE), F...  87.7 us
    unnamed x2, local copies, waits for them, and re-layouts  3.44 us

profile of v3, /device:TPU:1, one launch (start us, length us, event | category | flops | bytes accessed | tf_op | source)
XLA Modules:
  0.0 91.8 jit_solution(14408022247152080425)
XLA Ops:
  0.6 87.7 %shard_map.77 = (f32[2,256,256]{2,1,0:T(8,128)}, f32[2,128,128]{2,1,0:T(8,128)}) custom-call(f32[2,256,256]{2,1,0:T(8,128)} %obj_in.1, f32[2,128,128]{2,1,0:T(8,128)} %probe_in.1, f32[2,1,1,16,128,128]{5,4,3,2,1,0:T(8,128)} %amp_in.1, s32[2,2,1,1,16]{4,3,2,1,0:T(1,128)} %pos_in.1, s32[2,2,1,1,16]{4,3,2,1,0:T(1,128)} %shf_in.1, ...), custom_call_target="tpu_custom_call" | custom-call | tf_op jit(solution)/shard_map/pallas_call | solution.py:488
  88.4 1.9 %copy.10 = f32[2,256,256]{2,1,0:T(8,128)} copy(f32[2,256,256]{2,1,0:T(8,128)} %get-tuple-element.4) | data formatting | bytes 1048576
  90.2 1.6 %copy.11 = f32[2,128,128]{2,1,0:T(8,128)} copy(f32[2,128,128]{2,1,0:T(8,128)} %get-tuple-element.5) | data formatting | bytes 262144

commit v4 on v3

--- a/solution.py
+++ b/solution.py
@@ -87,6 +87,7 @@
 
     partner = (r + 1 - 2 * core, c)
     around = [(-1, 0), (1, 0), (0, -1), (0, 1), (-1, -1), (-1, 1), (1, -1), (1, 1), (-1, 0), (1, 0)]
+    around += [(0, -1), (0, 1), (0, -1), (0, 1)]
 
     barrier = pltpu.get_barrier_semaphore()
     peers = [near(*d) for d in around[:8]]
@@ -154,17 +155,23 @@
             remote(src[i], dst[i], halo_s.at[h, i], halo_r.at[h, i], near(*around[i])) for i in range(10)
         ]
 
-    def halo_send(h, copies, j):
-        for t in (0, 3, 1, 2):
-            rows = slice(HALF + 64 * t, HALF + 64 * t + 64)
-            to = slice(64 * t, 64 * t + 64)
-            re, im = obj[0, j, rows], obj[1, j, rows]
-            if j == 1:
-                hpack[h, 0, to] = jnp.where(low_half, re, pltpu.roll(im, 64, 1))
-            else:
-                hpack[h, 1, to] = jnp.where(low_half, pltpu.roll(re, 64, 1), im)
-            if t == 3:
-                start(copies, (4, 6, 0, 1) if j == 1 else (5, 7, 8, 9))
+    def halo_pack(h, j, t):
+        rows = slice(HALF + 64 * t, HALF + 64 * t + 64)
+        to = slice(64 * t, 64 * t + 64)
+        re, im = obj[0, j, rows], obj[1, j, rows]
+        if j == 1:
+            hpack[h, 0, to] = jnp.where(low_half, re, pltpu.roll(im, 64, 1))
+        else:
+            hpack[h, 1, to] = jnp.where(low_half, pltpu.roll(re, 64, 1), im)
+
+    def halo_edges(h, copies, j):
+        for t in (0, 3):
+            halo_pack(h, j, t)
+        start(copies, (4, 6, 0, 1) if j == 1 else (5, 7, 8, 9))
+
+    def halo_sides(h, copies, j):
+        for t in (1, 2):
+            halo_pack(h, j, t)
         start(copies, (2,) if j == 1 else (3,))
 
     def halo_finish(h, copies):
@@ -248,84 +255,76 @@
         terms[0:128] = q_re
         terms[128:256] = q_im
 
-    def gather_gradient(it, j, t):
-        def add(b, acc):
-            u, k, s = place_of(it, b)
-            start = CENTRE - u + 64 * t
-            low = jnp.where(k == j, s, WIDTH)
-            high = jnp.where(k + 1 == j, s, 0)
-            mine = jnp.logical_or(lane >= low, lane < high)
-            return tuple(
-                acc[part] + jnp.where(mine, zb[b, part, pl.ds(start, 64), :], 0.0) for part in range(2)
-            )
-
-        zero = jnp.zeros((64, WIDTH), F32)
-        re, im = lax.fori_loop(0, BATCH, add, (zero, zero), unroll=4)
-        if isinstance(t, int):
-            rows = slice(64 * t, 64 * t + 64)
-        else:
-            rows = pl.ds(pl.multiple_of(64 * t, 64), 64)
-        grad[0, j, rows] = re
-        grad[1, j, rows] = im
-        return re, im
+    def gather_gradient(it, t):
+        rows = slice(64 * t, 64 * t + 64) if isinstance(t, int) else pl.ds(pl.multiple_of(64 * t, 64), 64)
+        for part in range(2):
+
+            def add(b, acc, part=part):
+                u, k, s = place_of(it, b)
+                placed = zb[b, part, pl.ds(CENTRE - u + 64 * t, 64), :]
+                out = []
+                for j in range(BLOCKS):
+                    low = jnp.where(k == j, s, WIDTH)
+                    high = jnp.where(k + 1 == j, s, 0)
+                    mine = jnp.logical_or(lane >= low, lane < high)
+                    out.append(acc[j] + jnp.where(mine, placed, 0.0))
+                return tuple(out)
+
+            zero = jnp.zeros((64, WIDTH), F32)
+            sums = lax.fori_loop(0, BATCH, add, (zero,) * BLOCKS, unroll=8)
+            for j in range(BLOCKS):
+                grad[part, j, rows] = sums[j]
+        pack[0, rows] = jnp.where(low_half, pltpu.roll(grad[0, 0, rows], 64, 1), grad[1, 0, rows])
+        pack[1, rows] = jnp.where(low_half, grad[0, 3, rows], pltpu.roll(grad[1, 3, rows], 64, 1))
 
     def fold_copies(it):
         src = [
-            grad.at[:, 1, 0:64], grad.at[:, 1, 320:384], pack.at[0, 64:320], pack.at[1, 64:320],
+            grad.at[:, 1, 0:64], grad.at[:, 1, 320:384], pack.at[0, 128:256], pack.at[1, 128:256],
             pack.at[0, 0:64], pack.at[1, 0:64], pack.at[0, 320:384], pack.at[1, 320:384],
             grad.at[:, 2, 0:64], grad.at[:, 2, 320:384],
+            pack.at[0, 64:128], pack.at[1, 64:128], pack.at[0, 256:320], pack.at[1, 256:320],
         ]
         dst = [
-            fold_row.at[0, 0], fold_row.at[1, 0], fold_col.at[0], fold_col.at[1],
+            fold_row.at[0, 0], fold_row.at[1, 0], fold_col.at[0, 64:192], fold_col.at[1, 64:192],
             fold_cor.at[0], fold_cor.at[1], fold_cor.at[2], fold_cor.at[3],
             fold_row.at[0, 1], fold_row.at[1, 1],
+            fold_col.at[0, 0:64], fold_col.at[1, 0:64], fold_col.at[0, 192:256], fold_col.at[1, 192:256],
         ]
         return [
-            remote(src[i], dst[i], fold_s.at[it, i], fold_r.at[it, i], near(*around[i])) for i in range(10)
+            remote(src[i], dst[i], fold_s.at[it, i], fold_r.at[it, i], near(*around[i])) for i in range(14)
         ]
-
-    def rim(it, t):
-        re, im = gather_gradient(it, 0, t)
-        rows = slice(64 * t, 64 * t + 64) if isinstance(t, int) else pl.ds(pl.multiple_of(64 * t, 64), 64)
-        pack[0, rows] = jnp.where(low_half, pltpu.roll(re, 64, 1), im)
-        re, im = gather_gradient(it, 3, t)
-        pack[1, rows] = jnp.where(low_half, re, pltpu.roll(im, 64, 1))
 
     def fold_send(it):
         copies = fold_copies(it)
-        for t, corners in ((0, (4, 5)), (5, (6, 7))):
-            rim(it, t)
-            start(copies, corners)
-        for j in (1, 2):
-            for t in (0, 5):
-                gather_gradient(it, j, t)
-                start(copies, [(0 if j == 1 else 8) + t // 5])
+        gather_gradient(it, 0)
+        start(copies, (4, 5, 0, 8))
+        gather_gradient(it, 5)
+        start(copies, (6, 7, 1, 9))
+        gather_gradient(it, 1)
+        gather_gradient(it, 4)
+        if it + 1 < ITERS:
+            start(copies, (10, 11, 12, 13))
 
         def middle(t, carry):
-            rim(it, t)
+            gather_gradient(it, t)
             return carry
 
-        lax.fori_loop(1, 5, middle, 0)
+        lax.fori_loop(2, 4, middle, 0)
         if it + 1 < ITERS:
             start(copies, (2, 3))
         return copies
 
-    def interior(it):
-        def rows(t, carry):
-            gather_gradient(it, 1, t)
-            gather_gradient(it, 2, t)
-            return carry
-
-        lax.fori_loop(1, 5, rows, 0)
-
-    def fold_finish(copies, step, j):
-        finish(copies, (0, 1, 3, 5, 7) if j == 1 else (8, 9, 2, 4, 6))
+    def fold_finish(copies, step, j, edges):
+        if edges:
+            finish(copies, (0, 1, 5, 7, 11, 13) if j == 1 else (8, 9, 4, 6, 10, 12))
+        else:
+            finish(copies, (3,) if j == 1 else (2,))
         up, down = inside(-1, 0), inside(1, 0)
         beside = inside(0, -1 if j == 1 else 1)
-        for t in range(4):
+        for t in (0, 3) if edges else (1, 2):
             rows = slice(HALF + 64 * t, HALF + 64 * t + 64)
             at = slice(64 * t, 64 * t + 64)
-            side = jnp.where(beside, fold_col[2 - j if j == 2 else 1, at], 0.0)
+            side = jnp.where(beside, fold_col[2 - j, at], 0.0)
             if t == 0:
                 side = side + jnp.where(jnp.logical_and(up, beside), fold_cor[3 if j == 1 else 2], 0.0)
             if t == 3:
@@ -389,15 +388,17 @@
             arriving = summed.at[it, chunk((xy + NX * NY - d) % (NX * NY))]
             remote(rows, arriving, out_s.at[it, d], out_r.at[it, d], at_xy(d)).wait()
         under = summed[it, 256:384] + 0.2 * PATTERNS
-        prb[0] = prb[0] - summed[it, 0:128] / under
-        prb[1] = prb[1] - summed[it, 128:256] / under
+        for part in range(2):
+            prb[part] = prb[part] - summed[it, part * 128:(part + 1) * 128] / under
 
     loads[0].wait()
     loads[1].wait()
     pl.semaphore_wait(barrier, len(peers))
     copies = halo_copies(0)
-    halo_send(0, copies, 1)
-    halo_send(0, copies, 2)
+    for j in (1, 2):
+        halo_edges(0, copies, j)
+    for j in (1, 2):
+        halo_sides(0, copies, j)
 
     def clear(b, carry):
         for part in range(2):
@@ -415,19 +416,14 @@
     for it in range(ITERS):
         terms[...] = jnp.zeros((TERM_ROWS, WIDTH), F32)
 
-        def some(g, carry):
-            patterns(it, g * 8, 4)
-            return carry
-
-        lax.fori_loop(0, BATCH // 8, some, 0)
+        patterns(it, 0, BATCH // 2)
+        summing = xy_scatter(it)
+        folds = fold_send(it)
         power = prb[0] * prb[0] + prb[1] * prb[1]
         step = 0.5 / (jnp.max(power) + 1e-6)
-        summing = xy_scatter(it)
-        folds = fold_send(it)
-        interior(it)
         z_gather(it, summing)
         if it + 1 == ITERS:
-            start(folds, (2, 3))
+            start(folds, (2, 3, 10, 11, 12, 13))
         if it + 1 < ITERS:
             copies = halo_copies(it + 1)
         else:
@@ -437,12 +433,16 @@
                 )
                 for j in range(2)
             ]
-        for j in (1, 2):
-            fold_finish(folds, step, j)
-            if it + 1 < ITERS:
-                halo_send(it + 1, copies, j)
-            else:
-                stores[j - 1].start()
+        for edges in (True, False):
+            for j in (1, 2):
+                fold_finish(folds, step, j, edges)
+                if it + 1 == ITERS:
+                    if not edges:
+                        stores[j - 1].start()
+                elif edges:
+                    halo_edges(it + 1, copies, j)
+                else:
+                    halo_sides(it + 1, copies, j)
         xy_gather(it)
         new_probe_from(it)
         if it + 1 < ITERS:
@@ -479,7 +479,7 @@
         pltpu.VMEM((ITERS, TERM_ROWS, WIDTH), F32),
         dma((10,)),
         dma((ITERS, 10)), dma((ITERS, 10)),
-        dma((ITERS, 10)), dma((ITERS, 10)),
+        dma((ITERS, 14)), dma((ITERS, 14)),
         dma((ITERS, NX * NY)), dma((ITERS, NX * NY)),
         dma((ITERS,)), dma((ITERS,)),
         dma((ITERS, NZ)), dma((ITERS, NZ)),

time: 91.9 us -> 89.9 us (0.978)
  Pallas kernels: 87.7 us -> 85.5 us
    pallas_call x1, Pallas kernels: 87.7 us -> 85.5 us  [local(): pl.pallas_call(kernel, out_shape=(jax.ShapeDtypeStruct((2, TILE, TILE), F...]
where the time goes in v4:
time: 89.9 us; the launch traced here: 89.6 us
  Pallas kernels  85.5 us (95%)
  local copies, waits for them, and re-layouts  3.44 us (4%)
    pallas_call x1, Pallas kernels, local(): pl.pallas_call(kernel, out_shape=(jax.ShapeDtypeStruct((2, TILE, TILE), F...  85.5 us
    unnamed x2, local copies, waits for them, and re-layouts  3.44 us

profile of v4, /device:TPU:1, one launch (start us, length us, event | category | flops | bytes accessed | tf_op | source)
XLA Modules:
  0.0 89.6 jit_solution(17381841834349215902)
XLA Ops:
  0.6 85.5 %shard_map.77 = (f32[2,256,256]{2,1,0:T(8,128)}, f32[2,128,128]{2,1,0:T(8,128)}) custom-call(f32[2,256,256]{2,1,0:T(8,128)} %obj_in.1, f32[2,128,128]{2,1,0:T(8,128)} %probe_in.1, f32[2,1,1,16,128,128]{5,4,3,2,1,0:T(8,128)} %amp_in.1, s32[2,2,1,1,16]{4,3,2,1,0:T(1,128)} %pos_in.1, s32[2,2,1,1,16]{4,3,2,1,0:T(1,128)} %shf_in.1, ...), custom_call_target="tpu_custom_call" | custom-call | tf_op jit(solution)/shard_map/pallas_call | solution.py:488
  86.1 1.9 %copy.10 = f32[2,256,256]{2,1,0:T(8,128)} copy(f32[2,256,256]{2,1,0:T(8,128)} %get-tuple-element.4) | data formatting | bytes 1048576
  88.0 1.6 %copy.11 = f32[2,128,128]{2,1,0:T(8,128)} copy(f32[2,128,128]{2,1,0:T(8,128)} %get-tuple-element.5) | data formatting | bytes 262144

commit v5 on v4

--- a/solution.py
+++ b/solution.py
@@ -433,6 +433,8 @@
                 )
                 for j in range(2)
             ]
+        if it + 1 == ITERS:
+            xy_gather(it)
         for edges in (True, False):
             for j in (1, 2):
                 fold_finish(folds, step, j, edges)
@@ -443,7 +445,8 @@
                     halo_edges(it + 1, copies, j)
                 else:
                     halo_sides(it + 1, copies, j)
-        xy_gather(it)
+        if it + 1 < ITERS:
+            xy_gather(it)
         new_probe_from(it)
         if it + 1 < ITERS:
             halo_finish(it + 1, copies)

time: 89.9 us -> 87.3 us (0.971)
  Pallas kernels: 85.5 us -> 82 us
    pallas_call x1, Pallas kernels: 85.5 us -> 82 us  [local(): pl.pallas_call(kernel, out_shape=(jax.ShapeDtypeStruct((2, TILE, TILE), F...]
where the time goes in v5:
time: 87.3 us; the launch traced here: 86.1 us
  Pallas kernels  82 us (94%)
  local copies, waits for them, and re-layouts  3.44 us (4%)
    pallas_call x1, Pallas kernels, local(): pl.pallas_call(kernel, out_shape=(jax.ShapeDtypeStruct((2, TILE, TILE), F...  82 us
    unnamed x2, local copies, waits for them, and re-layouts  3.44 us

profile of v5, /device:TPU:1, one launch (start us, length us, event | category | flops | bytes accessed | tf_op | source)
XLA Modules:
  0.0 86.1 jit_solution(12219313968269660759)
XLA Ops:
  0.6 82.0 %shard_map.77 = (f32[2,256,256]{2,1,0:T(8,128)}, f32[2,128,128]{2,1,0:T(8,128)}) custom-call(f32[2,256,256]{2,1,0:T(8,128)} %obj_in.1, f32[2,128,128]{2,1,0:T(8,128)} %probe_in.1, f32[2,1,1,16,128,128]{5,4,3,2,1,0:T(8,128)} %amp_in.1, s32[2,2,1,1,16]{4,3,2,1,0:T(1,128)} %pos_in.1, s32[2,2,1,1,16]{4,3,2,1,0:T(1,128)} %shf_in.1, ...), custom_call_target="tpu_custom_call" | custom-call | tf_op jit(solution)/shard_map/pallas_call | solution.py:491
  82.7 1.9 %copy.10 = f32[2,256,256]{2,1,0:T(8,128)} copy(f32[2,256,256]{2,1,0:T(8,128)} %get-tuple-element.4) | data formatting | bytes 1048576
  84.5 1.6 %copy.11 = f32[2,128,128]{2,1,0:T(8,128)} copy(f32[2,128,128]{2,1,0:T(8,128)} %get-tuple-element.5) | data formatting | bytes 262144
